TPU v7x, 32 devices: a whole 2x2x4 slice. The times are simulated.
32 devices in a mesh: ctx: 8 (over z, x), fsdp: 4 (over y, core).
Axes of the slice: x: 2, y: 2, z: 4, core: 2. Of those that a mesh axis runs over, the one named last changes fastest.
Arguments:
- tokens: bfloat16 [4, 2048, 1280], P('fsdp', 'ctx'), may hold values from -6 to 6
- lengths: int32 [4, 4], P('fsdp'), may hold values from 1 to 1024, 1920 in all within a row
- position: int32 [4, 2048], P('fsdp'), may hold values from 0 to 2047, as said below
- qkv_weight: bfloat16 [1280, 3840], P('fsdp'), may hold values from -0.15625 to 0.15625
- out_weight: bfloat16 [1280, 1280], P('fsdp'), may hold values from -0.5 to 0.5
- up_weight: bfloat16 [1280, 1280], P('fsdp'), may hold values from -0.15625 to 0.15625
- down_weight: bfloat16 [1280, 1280], P('fsdp'), may hold values from -0.15625 to 0.15625
- attn_gain: bfloat16 [1280], P('fsdp'), may hold values from 0.099609375 to 1.8984375
- mlp_gain: bfloat16 [1280], P('fsdp'), may hold values from 0.099609375 to 1.8984375
- query_scale: bfloat16 [80], P('fsdp'), may hold values from -3 to 3
- cotangent: bfloat16 [4, 2048, 1280], P('fsdp', 'ctx'), may hold values from -6 to 6
Outputs:
- output: float32 [4, 2048, 1280], P('fsdp', 'ctx')
- input_grad: float32 [4, 2048, 1280], P('fsdp', 'ctx')
- grad_qkv: float32 [1280, 3840], P('fsdp')
- grad_out: float32 [1280, 1280], P('fsdp')
- grad_up: float32 [1280, 1280], P('fsdp')
- grad_down: float32 [1280, 1280], P('fsdp')
- grad_attn_gain: float32 [1280], P('fsdp')
- grad_mlp_gain: float32 [1280], P('fsdp')
- grad_query_scale: float32 [80], P('fsdp')
Inputs may be any that keep to these rules, and one draw needn't show every extreme that they name: Each pack's sequences fill positions from 0 in order; positions from the sum of the lengths to the end are padding. Each row of position is a permutation of the pack's positions, and every run of 256 given rows of one index of ctx holds exactly 256 // 8 positions of each residue modulo 8.
All inputs are finite; a program needn't handle non-finite values.
Results may differ from a plain program's by a relative error of at most 0.04.
Values may be sent and summed in bfloat16 or wider, within the bound.
A program may use at most 256 MiB of HBM per device.

v0:
```python
import functools
import math

import jax
import jax.numpy as jnp
from jax import lax
from jax.experimental import pallas as pl
from jax.experimental.pallas import tpu as pltpu
from jax.sharding import PartitionSpec as P

HEADS = 16


EPS = 1e-06
FLOOR = -1e30
LOG2E = 1.442695041

MESH = pl.DeviceIdType.MESH
LANES = 128
BF = jnp.bfloat16
F32 = jnp.float32
VMEM_SPEC = pl.BlockSpec(memory_space=pltpu.VMEM)
ANY_SPEC = pl.BlockSpec(memory_space=pl.ANY)
VMEM_LIMIT = 60 << 20


def flip(number, mask):
    total = 0
    for bit in (1, 2, 4):
        left = (number // bit) % 2
        right = (mask // bit) % 2
        total = total + bit * (left + right - 2 * left * right)
    return total


class Place:
    def __init__(self):
        self.c = lax.axis_index("ctx")
        self.f = lax.axis_index("fsdp")
        self.core = self.f % 2
        self.plane = self.f - self.core
        self.half = self.c // 4
        self.pack = self.plane + self.half
        self.group = (self.c % 4) * 2 + self.core
        self.twin = self.plane + 1 - self.core
        self.across = (self.f + 2) % 4


def dev(ctx, fsdp):
    return {"ctx": ctx, "fsdp": fsdp}


def send(src, dst, send_sem, recv_sem, device):
    copy = pltpu.make_async_remote_copy(
        src_ref=src,
        dst_ref=dst,
        send_sem=send_sem,
        recv_sem=recv_sem,
        device_id=device,
        device_id_type=MESH,
    )
    copy.start()
    return copy


def await_recv(ref, sem):
    pltpu.make_async_copy(ref, ref, sem).wait()


def meet_plane(at):
    barrier = pltpu.get_barrier_semaphore()

    def greet(k, carry):
        pl.semaphore_signal(
            barrier,
            1,
            device_id=dev((at.c + k // 2) % 8, at.plane + (at.core + k) % 2),
            device_id_type=MESH,
        )
        return carry

    lax.fori_loop(1, 16, greet, 0)
    for k in range(2):
        pl.semaphore_signal(
            barrier, 1, device_id=dev(at.c, (at.plane + 2) % 4 + k), device_id_type=MESH
        )
    pl.semaphore_wait(barrier, 17)


def span(start, size, unit):
    return pl.ds(pl.multiple_of(start, unit), size)


def doc_index(places, seq_ends):
    return jnp.sum((places[:, None] >= seq_ends[None, :]).astype(jnp.int32), axis=1)


def spread_position(gathered_index, tok_dev, cycle_size):
    return gathered_index % tok_dev * cycle_size + gathered_index // tok_dev


def pair_scores(left_rows, right_rows):
    return jnp.einsum(
        "qhd,khd->qhk",
        left_rows.reshape(left_rows.shape[0], HEADS, -1),
        right_rows.reshape(right_rows.shape[0], HEADS, -1),
        preferred_element_type=jnp.float32,
    )


def pair_mask(query_pos, query_doc, key_pos, key_doc):
    return ((query_doc[:, None] == key_doc[None, :]) & (key_pos[None, :] <= query_pos[:, None]))[
        :, None, :
    ]


def in_blocks(advance, carried, pieces):
    total_rows = pieces[0].shape[0]
    block_rows = math.gcd(total_rows, 1024)
    block_count = total_rows // block_rows
    split = tuple((p.reshape((block_count, block_rows) + p.shape[1:]) for p in pieces))

    def inner(running, entry):
        return (advance(running, entry[1], entry[0] * block_rows), None)

    result, unused = lax.scan(inner, carried, (jnp.arange(block_count, dtype=jnp.int32), split))
    return result


def pair_terms(
    query_part,
    grad_part,
    log_part,
    delta_part,
    query_pos,
    query_doc,
    key_part,
    value_part,
    key_pos,
    key_doc,
):
    visible = pair_mask(query_pos, query_doc, key_pos, key_doc)
    prob_float = jnp.where(
        visible, jnp.exp(pair_scores(query_part, key_part) - log_part[:, :, None]), 0.0
    )
    grad_probs = pair_scores(grad_part, value_part)
    score_grad = (prob_float * (grad_probs - delta_part[:, :, None])).astype(jnp.bfloat16)
    return (prob_float.astype(jnp.bfloat16), score_grad)


def body(
    tokens,
    lengths,
    position,
    qkv_weight,
    out_weight,
    up_weight,
    down_weight,
    attn_gain,
    mlp_gain,
    query_scale,
    cotangent,
):
    cycle_size = lax.axis_size("ctx")
    my_index = lax.axis_index("ctx")
    tok_dev = tokens.shape[1]
    share_rows = tok_dev // cycle_size
    seq_ends = jnp.cumsum(lengths[0])
    place_row = position[0]
    residue = (place_row % cycle_size).reshape(cycle_size, tok_dev)
    landing = place_row // cycle_size
    matches = (
        residue[:, :, None] == jnp.arange(cycle_size, dtype=jnp.int32)[None, None, :]
    ).astype(jnp.int32)
    ranked = jnp.sum(jnp.cumsum(matches, axis=1) * matches, axis=2) - 1
    buffer_slot = residue * share_rows + ranked
    my_slots = lax.dynamic_index_in_dim(buffer_slot, my_index, 0, keepdims=False)
    local_rows = jnp.arange(tok_dev, dtype=jnp.int32)
    outgoing = jnp.zeros((tok_dev,), jnp.int32).at[my_slots].set(local_rows)
    flat_slot = (jnp.arange(cycle_size, dtype=jnp.int32)[:, None] * tok_dev + buffer_slot).reshape(
        -1
    )
    landing_table = (
        jnp.zeros((cycle_size * tok_dev,), jnp.int32)
        .at[flat_slot]
        .set(landing)
        .reshape(cycle_size, cycle_size, share_rows)
    )
    arrived_slot = lax.dynamic_index_in_dim(landing_table, my_index, 1, keepdims=False).reshape(-1)
    arrived_order = jnp.zeros((tok_dev,), jnp.int32).at[arrived_slot].set(local_rows)
    moved_x, moved_dy = (
        lax.all_to_all(tokens[0][outgoing], "ctx", split_axis=0, concat_axis=0, tiled=True),
        lax.all_to_all(cotangent[0][outgoing], "ctx", split_axis=0, concat_axis=0, tiled=True),
    )
    dealt_x = moved_x[arrived_order]
    dealt_dy = moved_dy[arrived_order]
    query_pos = local_rows * cycle_size + my_index
    query_doc = doc_index(query_pos, seq_ends)
    full_qkv, full_out, full_up, full_down, attn_gain_full, mlp_gain_full, scale_full = (
        lax.all_gather(qkv_weight, "fsdp", axis=0, tiled=True),
        lax.all_gather(out_weight, "fsdp", axis=0, tiled=True),
        lax.all_gather(up_weight, "fsdp", axis=0, tiled=True),
        lax.all_gather(down_weight, "fsdp", axis=0, tiled=True),
        lax.all_gather(attn_gain, "fsdp", axis=0, tiled=True),
        lax.all_gather(mlp_gain, "fsdp", axis=0, tiled=True),
        lax.all_gather(query_scale, "fsdp", axis=0, tiled=True),
    )
    attn_gain_f = attn_gain_full.astype(jnp.float32)
    mlp_gain_f = mlp_gain_full.astype(jnp.float32)
    scale_float = scale_full.astype(jnp.float32)
    x_float = dealt_x.astype(jnp.float32)
    inv_attn = lax.rsqrt(jnp.mean(x_float * x_float, axis=1, keepdims=True) + EPS)
    normed_attn = (x_float * inv_attn * attn_gain_f).astype(jnp.bfloat16)
    projected = jnp.dot(normed_attn, full_qkv, preferred_element_type=jnp.float32)
    att_width = projected.shape[1] // 3
    head_dim = scale_full.shape[0]
    base_scale = LOG2E / math.sqrt(head_dim)
    multiplier = jnp.tile(base_scale * jax.nn.softplus(scale_float), att_width // head_dim)
    raw_query = projected[:, :att_width]
    queries = (raw_query * multiplier).astype(jnp.bfloat16)
    key_rows = projected[:, att_width : 2 * att_width].astype(jnp.bfloat16)
    value_rows = projected[:, 2 * att_width :].astype(jnp.bfloat16)

    def key_place(first_row, amount):
        gathered_index = first_row + jnp.arange(amount, dtype=jnp.int32)
        key_pos = spread_position(gathered_index, tok_dev, cycle_size)
        return (key_pos, doc_index(key_pos, seq_ends))

    def stat_block(carried, pieces, first_row):
        running_max, running_sum = carried
        key_pos, key_doc = key_place(first_row, pieces[0].shape[0])
        visible = pair_mask(query_pos, query_doc, key_pos, key_doc)
        logits = jnp.where(visible, pair_scores(queries, pieces[0]), FLOOR)
        new_max = jnp.maximum(running_max, jnp.max(logits, axis=2))
        added = jnp.sum(jnp.where(visible, jnp.exp(logits - new_max[:, :, None]), 0.0), axis=2)
        return (new_max, running_sum * jnp.exp(running_max - new_max) + added)

    def output_block(summed, pieces, first_row):
        key_pos, key_doc = key_place(first_row, pieces[0].shape[0])
        visible = pair_mask(query_pos, query_doc, key_pos, key_doc)
        prob_low = jnp.where(
            visible, jnp.exp(pair_scores(queries, pieces[0]) - log_total[:, :, None]), 0.0
        ).astype(jnp.bfloat16)
        values_part = pieces[1].reshape(pieces[1].shape[0], HEADS, -1)
        return summed + jnp.einsum(
            "qhk,khd->qhd", prob_low, values_part, preferred_element_type=jnp.float32
        ).reshape(summed.shape)

    def query_grad_block(summed, pieces, first_row):
        key_pos, key_doc = key_place(first_row, pieces[0].shape[0])
        unused_probs, score_grad = pair_terms(
            queries,
            attended_grad,
            log_total,
            row_delta,
            query_pos,
            query_doc,
            pieces[0],
            pieces[1],
            key_pos,
            key_doc,
        )
        keys_part = pieces[0].reshape(pieces[0].shape[0], HEADS, -1)
        return summed + jnp.einsum(
            "qhk,khd->qhd", score_grad, keys_part, preferred_element_type=jnp.float32
        ).reshape(summed.shape)

    def key_grad_block(carried, pieces, first_row):
        amount = pieces[0].shape[0]
        part_pos, part_doc = key_place(first_row, amount)
        part_log = lax.dynamic_slice_in_dim(all_log, first_row, amount, 0)
        part_delta = lax.dynamic_slice_in_dim(all_delta, first_row, amount, 0)
        prob_low, score_grad = pair_terms(
            pieces[0],
            pieces[1],
            part_log,
            part_delta,
            part_pos,
            part_doc,
            key_rows,
            value_rows,
            query_pos,
            query_doc,
        )
        grad_keys = carried[0] + jnp.einsum(
            "qhk,qhd->khd",
            score_grad,
            pieces[0].reshape(amount, HEADS, -1),
            preferred_element_type=jnp.float32,
        ).reshape(tok_dev, -1)
        grad_values = carried[1] + jnp.einsum(
            "qhk,qhd->khd",
            prob_low,
            pieces[1].reshape(amount, HEADS, -1),
            preferred_element_type=jnp.float32,
        ).reshape(tok_dev, -1)
        return (grad_keys, grad_values)

    zero_stats = (
        jnp.full((tok_dev, HEADS), FLOOR, jnp.float32),
        jnp.zeros((tok_dev, HEADS), jnp.float32),
    )
    zero_rows = jnp.zeros((tok_dev, att_width), jnp.float32)
    running_max, running_sum = in_blocks(
        stat_block, zero_stats, (lax.all_gather(key_rows, "ctx", axis=0, tiled=True),)
    )
    log_total = running_max + jnp.log(running_sum)
    attended = in_blocks(
        output_block,
        zero_rows,
        (
            lax.all_gather(key_rows, "ctx", axis=0, tiled=True),
            lax.all_gather(value_rows, "ctx", axis=0, tiled=True),
        ),
    )
    attended_low = attended.astype(jnp.bfloat16)
    resid = x_float + jnp.dot(attended_low, full_out, preferred_element_type=jnp.float32)
    inv_mlp = lax.rsqrt(jnp.mean(resid * resid, axis=1, keepdims=True) + EPS)
    normed_mlp = (resid * inv_mlp * mlp_gain_f).astype(jnp.bfloat16)
    up_proj = jnp.dot(normed_mlp, full_up, preferred_element_type=jnp.float32)
    act_low = jax.nn.silu(up_proj).astype(jnp.bfloat16)
    result = resid + jnp.dot(act_low, full_down, preferred_element_type=jnp.float32)
    cot_float = dealt_dy.astype(jnp.float32)
    grad_down = jnp.dot(act_low.T, dealt_dy, preferred_element_type=jnp.float32)
    act_grad = jnp.dot(dealt_dy, full_down.T, preferred_element_type=jnp.float32)
    sigma = jax.nn.sigmoid(up_proj)
    up_grad = (act_grad * sigma * (1.0 + up_proj * (1.0 - sigma))).astype(jnp.bfloat16)
    grad_up = jnp.dot(normed_mlp.T, up_grad, preferred_element_type=jnp.float32)
    norm_mlp_grad = jnp.dot(up_grad, full_up.T, preferred_element_type=jnp.float32)
    grad_mlp_gain = jnp.sum(norm_mlp_grad * resid * inv_mlp, axis=0)
    scaled_mlp = norm_mlp_grad * mlp_gain_f
    resid_grad = cot_float + inv_mlp * (
        scaled_mlp - resid * inv_mlp * inv_mlp * jnp.mean(scaled_mlp * resid, axis=1, keepdims=True)
    )
    branch_grad = resid_grad.astype(jnp.bfloat16)
    grad_out = jnp.dot(attended_low.T, branch_grad, preferred_element_type=jnp.float32)
    attended_grad = jnp.dot(branch_grad, full_out.T, preferred_element_type=jnp.float32).astype(
        jnp.bfloat16
    )
    row_delta = jnp.sum(
        (attended_grad.astype(jnp.float32) * attended).reshape(tok_dev, HEADS, -1), axis=2
    )
    query_grads = in_blocks(
        query_grad_block,
        zero_rows,
        (
            lax.all_gather(key_rows, "ctx", axis=0, tiled=True),
            lax.all_gather(value_rows, "ctx", axis=0, tiled=True),
        ),
    )
    all_log, all_delta = (
        lax.all_gather(log_total, "ctx", axis=0, tiled=True),
        lax.all_gather(row_delta, "ctx", axis=0, tiled=True),
    )
    key_grad_f, value_grad_f = in_blocks(
        key_grad_block,
        (zero_rows, zero_rows),
        (
            lax.all_gather(queries, "ctx", axis=0, tiled=True),
            lax.all_gather(attended_grad, "ctx", axis=0, tiled=True),
        ),
    )
    scale_terms = jnp.sum((query_grads * raw_query).reshape(tok_dev, -1, head_dim), axis=(0, 1))
    grad_scale = scale_terms * base_scale * jax.nn.sigmoid(scale_float)
    proj_grad = jnp.concatenate(
        [
            (query_grads * multiplier).astype(jnp.bfloat16),
            key_grad_f.astype(jnp.bfloat16),
            value_grad_f.astype(jnp.bfloat16),
        ],
        axis=1,
    )
    grad_qkv = jnp.dot(normed_attn.T, proj_grad, preferred_element_type=jnp.float32)
    norm_attn_grad = jnp.dot(proj_grad, full_qkv.T, preferred_element_type=jnp.float32)
    grad_attn_gain = jnp.sum(norm_attn_grad * x_float * inv_attn, axis=0)
    scaled_attn = norm_attn_grad * attn_gain_f
    input_grad = resid_grad + inv_attn * (
        scaled_attn
        - x_float * inv_attn * inv_attn * jnp.mean(scaled_attn * x_float, axis=1, keepdims=True)
    )
    owned = (
        lax.psum_scatter(grad_qkv, "fsdp", scatter_dimension=0, tiled=True),
        lax.psum_scatter(grad_out, "fsdp", scatter_dimension=0, tiled=True),
        lax.psum_scatter(grad_up, "fsdp", scatter_dimension=0, tiled=True),
        lax.psum_scatter(grad_down, "fsdp", scatter_dimension=0, tiled=True),
        lax.psum_scatter(grad_attn_gain, "fsdp", scatter_dimension=0, tiled=True),
        lax.psum_scatter(grad_mlp_gain, "fsdp", scatter_dimension=0, tiled=True),
        lax.psum_scatter(grad_scale, "fsdp", scatter_dimension=0, tiled=True),
    )
    summed_grads = lax.psum(
        (owned[0], owned[1], owned[2], owned[3], owned[4], owned[5], owned[6]), "ctx"
    )
    back_out, back_grad = (
        lax.all_to_all(result[arrived_slot], "ctx", split_axis=0, concat_axis=0, tiled=True),
        lax.all_to_all(input_grad[arrived_slot], "ctx", split_axis=0, concat_axis=0, tiled=True),
    )
    return (
        back_out[my_slots][None],
        back_grad[my_slots][None],
        summed_grads[0],
        summed_grads[1],
        summed_grads[2],
        summed_grads[3],
        summed_grads[4],
        summed_grads[5],
        summed_grads[6],
    )


HUB_WAYS = {k: ((2, 0), (2, 1)) for k in range(1, 8)}
HUB_WAYS[1] += ((1, 0),)
HUB_WAYS[2] += ((0, 1),)
HUB_WAYS[4] += ((0, 0), (0, 1), (1, 0), (1, 1))
HUB_WAYS[6] += ((0, 0), (0, 1))

SPLIT = (False, True, False)
WEIGHT_STEPS = ((2, 2, 1), (4, 2, 0), (6, 3, 1))


def attend_kernel(
    ends_ref,
    x_ref,
    w_ref,
    aux_ref,
    pos_ref,
    out_w_ref,
    up_w_ref,
    down_w_ref,
    dy_ref,
    att_ref,
    normed_out,
    qkv_out,
    lse_ref,
    out_ref,
    auxsum_ref,
    place_ref,
    w_out,
    result_ref,
    resid_grad_ref,
    branch_ref,
    up_grad_ref,
    act_ref,
    normed_mlp_ref,
    grad_ref,
    x_mine,
    w_mine,
    dy_mine,
    x_all,
    normed_ref,
    qkv_ref,
    w_all,
    w_own,
    w_small,
    weights,
    aux_all,
    pos_all,
    v_turned,
    key_pos,
    att_send,
    x_send_sem,
    x_recv_sem,
    w_send_sem,
    w_recv_sem,
    aux_send_sem,
    aux_recv_sem,
    pos_sem,
    att_send_sem,
    att_recv_sem,
    m_send_sem,
    m_recv_sem,
    local_sem,
    save_sem,
    shard_sem,
):
    w_load = pltpu.make_async_copy(w_ref, w_mine, local_sem.at[0])
    w_load.start()
    x_load = pltpu.make_async_copy(x_ref, x_mine, local_sem.at[2])
    dy_load = pltpu.make_async_copy(dy_ref, dy_mine, local_sem.at[4])
    at = Place()
    meet_plane(at)
    c, f = at.c, at.f
    hub = at.core == at.half

    aux_own = pltpu.make_async_copy(aux_ref, aux_all.at[f], local_sem.at[1])
    aux_own.start()
    x_own = pltpu.make_async_copy(x_ref, x_all.at[c], local_sem.at[3])

    halves = (pl.ds(0, 128), pl.ds(128, 128))

    def x_far(part):
        return pltpu.make_async_remote_copy(
            src_ref=x_ref.at[halves[part]],
            dst_ref=x_all.at[c, halves[part]],
            send_sem=x_send_sem.at[0, 0, part],
            recv_sem=x_recv_sem.at[c, part],
            device_id=dev(flip(c, 4), f),
            device_id_type=MESH,
        )

    @pl.when(hub)
    def _():
        x_own.start()
        for part in range(2):
            for k, where in enumerate((dev(flip(c, 1), f), dev(flip(c, 2), f), dev(c, at.twin))):
                send(
                    x_ref.at[halves[part]],
                    x_all.at[c, halves[part]],
                    x_send_sem.at[0, k, part],
                    x_recv_sem.at[c, part],
                    where,
                )

    @pl.when(jnp.logical_not(hub))
    def _():
        x_far(0).start()
        x_far(1).start()

    w_copies, aux_copies = [], []
    for k in (2, 1, 3):
        aux_copies.append(
            send(
                aux_ref,
                aux_all.at[f],
                aux_send_sem.at[k],
                aux_recv_sem.at[f],
                dev(c, (f + k) % 4),
            )
        )

    pos = pos_ref[...]
    start = jnp.zeros_like(pos)
    end = 0
    for k in range(4):
        end = end + ends_ref[0, k]
        start = jnp.where(pos >= end, end, start)
    pos_all[at.core, 0:1, :] = pos.astype(F32)
    pos_all[at.core, 1:2, :] = start.astype(F32)
    pos_all[at.core, 2:8, :] = jnp.zeros((6, 2048), F32)
    pos_copy = send(
        pos_all.at[at.core], pos_all.at[at.core], pos_sem.at[0], pos_sem.at[1], dev(c, at.twin)
    )

    row = lax.broadcasted_iota(jnp.int32, (1280, 512), 0)
    column = lax.broadcasted_iota(jnp.int32, (1280, 512), 1)
    first = (c % 4) * 320
    w_load.wait()
    for k in range(2):
        some = jnp.zeros((320, 512), F32)
        for j in range(3):
            pick = (row - first - k * 160 == column - j * 160) & (column // 160 == j)
            pick = jnp.where(pick, 1.0, 0.0).astype(BF)
            some += jnp.dot(w_mine[:, j * 1280 : (j + 1) * 1280], pick, preferred_element_type=F32)
        w_own[k] = some.astype(BF)
    mine_rows = span(f * 320, 320, 320)
    for k in (2, 3, 1):
        to = (f + k) % 4
        w_copies.append(
            send(
                w_own.at[to % 2],
                w_small.at[mine_rows],
                w_send_sem.at[k],
                w_recv_sem.at[f],
                dev(c, to),
            )
        )
    w_small[mine_rows, :] = w_own[at.core]
    x_load.start()
    dy_load.start()


    shards = (out_w_ref, up_w_ref, down_w_ref)
    xbit = c % 2
    other = (f + 2) % 4

    def part(m, owner, x):
        return weights.at[m, span(owner * 320 + x * 160, 160, 160)]

    def weight_copy(m, way):
        if way == 0:
            src, dst, to = shards[m], weights.at[m, mine_rows], dev(c, at.twin)
        elif way == 1 and not SPLIT[m]:
            src, dst, to = shards[m], weights.at[m, mine_rows], dev(c, other)
        elif way == 3 and not SPLIT[m]:
            src = dst = weights.at[m, span(other * 320, 320, 320)]
            to = dev(c, at.twin)
        elif way == 1:
            src = shards[m].at[span(xbit * 160, 160, 160)]
            dst, to = part(m, f, xbit), dev(c, other)
        else:
            x = (xbit, xbit, 1 - xbit)[way - 2]
            src = dst = part(m, other, x)
            to = (dev(flip(c, 1), f), dev(c, at.twin), dev(c, at.twin))[way - 2]
        return pltpu.make_async_remote_copy(
            src_ref=src,
            dst_ref=dst,
            send_sem=m_send_sem.at[m, way],
            recv_sem=m_recv_sem.at[m, way],
            device_id=to,
            device_id_type=MESH,
        )

    def shard_copy(m):
        return pltpu.make_async_copy(shards[m], weights.at[m, mine_rows], shard_sem.at[m])

    def weight_first(m):
        weight_copy(m, 0).start()
        weight_copy(m, 1).start()
        shard_copy(m).start()

    def weight_second(m):
        weight_copy(m, 1).wait_recv()
        if SPLIT[m]:
            weight_copy(m, 2).start()
        weight_copy(m, 3).start()

    def weight_third(m):
        if SPLIT[m]:
            weight_copy(m, 2).wait_recv()
            weight_copy(m, 4).start()

    def weight_last(m):
        shard_copy(m).wait()
        for way in (0, 3, 4) if SPLIT[m] else (0, 3):
            weight_copy(m, way).wait_recv()


    aux_own.wait()
    for k in (1, 2, 3):
        await_recv(aux_all.at[0], aux_recv_sem.at[(f + k) % 4])
    aux = jnp.zeros((16, 1280), F32)
    scale = jnp.zeros((16, LANES), F32)
    row = lax.broadcasted_iota(jnp.int32, (384, 1280), 0)
    column = lax.broadcasted_iota(jnp.int32, (384, 1280), 1)
    for k in range(4):
        put = jnp.where((column == row + k * 320) & (row < 320), 1.0, 0.0).astype(BF)
        aux = aux + jnp.dot(aux_all[k], put, preferred_element_type=F32)
        put = (column[:LANES, :LANES] == row[:LANES, :LANES] + k * 20) & (row[:LANES, :LANES] < 20)
        put = jnp.where(put, 1.0, 0.0).astype(BF)
        scale = scale + jnp.dot(aux_all[k, :, :LANES], put, preferred_element_type=F32)
    auxsum_ref[...] = aux
    auxsum_ref[2:3, :LANES] = scale[2:3]
    gain = aux[0:1, :]
    mlp_gain = aux[1:2, :]
    scale = scale[2:3]
    real = lax.broadcasted_iota(jnp.int32, (1, LANES), 1) < 80
    mult = jnp.where(
        real, LOG2E / math.sqrt(80) * (jnp.maximum(scale, 0.0) + jnp.log1p(jnp.exp(-jnp.abs(scale)))), 0.0
    )
    one = jnp.ones_like(mult)
    mults = jnp.concatenate([mult, mult, one, one, one, one], axis=1)

    await_recv(pos_all.at[0], pos_sem.at[1])
    place_ref[...] = pos_all[at.half]
    for k in range(8):
        block = place_ref[0:1, k * 256 : (k + 1) * 256]
        key_pos[k * 256 : (k + 1) * 256, :] = jnp.transpose(
            jnp.broadcast_to(block, (LANES, 256))
        )

    def arrive(step, carry):
        k = step + jnp.where(step == 3, 1, 0) - jnp.where(step == 4, 1, 0)
        slot = flip(c, k)
        for part in range(2):
            piece = x_all.at[slot, halves[part]]
            if part == 0:

                @pl.when(jnp.logical_and(hub, k == 0))
                def _():
                    x_own.wait()

            @pl.when(jnp.logical_not(jnp.logical_and(hub, k == 0)))
            def _(part=part, piece=piece):
                await_recv(piece, x_recv_sem.at[slot, part])

            def onward(way, where, part=part, piece=piece):
                send(
                    piece, piece, x_send_sem.at[k, way, part], x_recv_sem.at[slot, part], where
                )

            for way, where in enumerate((dev(flip(c, 1), f), dev(flip(c, 2), f), dev(c, at.twin))):
                due = False
                for when in HUB_WAYS:
                    if (way, part) in HUB_WAYS[when]:
                        due = jnp.logical_or(due, k == when)

                @pl.when(jnp.logical_and(hub, due))
                def _(way=way, where=where, onward=onward):
                    onward(way, where)

        @pl.when(step == 3)
        def _():
            weight_first(0)

        @pl.when(step == 5)
        def _():
            weight_first(1)


        xf = x_all[slot].astype(F32)
        inv = lax.rsqrt(jnp.mean(xf * xf, axis=1, keepdims=True) + EPS)
        rows = span(slot * 256, 256, 256)
        normed_ref[rows, :] = (xf * inv * gain).astype(BF)
        pltpu.make_async_copy(
            normed_ref.at[rows], normed_out.at[rows], save_sem.at[slot, 0]
        ).start()
        return carry

    def project(step, carry):
        slot = flip(c, step)
        rows = span(slot * 256, 256, 256)
        proj = jnp.dot(normed_ref[rows, :], w_all[...], preferred_element_type=F32)
        qkv_ref[rows, :] = (proj * mults).astype(BF)
        pltpu.make_async_copy(qkv_ref.at[rows], qkv_out.at[rows], save_sem.at[slot, 1]).start()
        return carry

    lax.fori_loop(0, 7, arrive, 0)
    for k in (1, 2, 3):
        await_recv(w_small.at[pl.ds(0, 320)], w_recv_sem.at[(f + k) % 4])
    weight_first(2)
    row = lax.broadcasted_iota(jnp.int32, (512, 768), 0)
    column = lax.broadcasted_iota(jnp.int32, (512, 768), 1)
    spread = (row == column // LANES * 80 + column % LANES) & (column % LANES < 80)
    spread = jnp.where(spread, 1.0, 0.0).astype(BF)
    w_all[...] = jnp.dot(w_small[...], spread, preferred_element_type=F32).astype(BF)
    w_save = pltpu.make_async_copy(w_all, w_out, local_sem.at[5])
    w_save.start()
    lax.fori_loop(0, 5, project, 0)
    lax.fori_loop(7, 8, arrive, 0)
    lax.fori_loop(5, 8, project, 0)

    for h in range(2):
        v_turned[h] = jnp.transpose(qkv_ref[:, (4 + h) * LANES : (5 + h) * LANES])

    att_own = pltpu.make_async_copy(
        att_send.at[c], att_ref.at[span(at.group * 160, 160, 160)], local_sem.at[3]
    )

    def att_copy(block):
        return pltpu.make_async_remote_copy(
            src_ref=att_send.at[block],
            dst_ref=att_ref.at[span(at.group * 160, 160, 160)],
            send_sem=att_send_sem.at[block],
            recv_sem=att_recv_sem.at[at.group],
            device_id=dev(block, at.pack),
            device_id_type=MESH,
        )

    mine = at.core == at.half

    def attend(step, carry):
        block = flip(c, 7 - step)
        lanes = span(block * 256, 256, 256)
        high = place_ref[0:1, lanes]
        least = place_ref[1:2, lanes]
        for h in range(2):
            query = qkv_ref[lanes, h * LANES : (h + 1) * LANES]
            scores, top = [], None
            for part in range(2):
                rows = slice(part * 1024, (part + 1) * 1024)
                kp = key_pos[rows, :]
                kp = jnp.concatenate([kp, kp], axis=1)
                keys = qkv_ref[rows, (2 + h) * LANES : (3 + h) * LANES]
                s = lax.dot_general(
                    keys, query, (((1,), (1,)), ((), ())), preferred_element_type=F32
                )
                s = jnp.where((kp >= least) & (kp <= high), s, FLOOR)
                scores.append(s)
                most = jnp.max(s, axis=0, keepdims=True)
                top = most if top is None else jnp.maximum(top, most)
            total = jnp.zeros((1, 256), F32)
            o = jnp.zeros((LANES, 256), F32)
            for part in range(2):
                p = jnp.exp(scores[part] - top)
                total += jnp.sum(p, axis=0, keepdims=True)
                values = v_turned[h, :, part * 1024 : (part + 1) * 1024]
                o += jnp.dot(values, p.astype(BF), preferred_element_type=F32)
            o = o[:80] / total
            lse_ref[h : h + 1, lanes] = top + jnp.log(total)
            out_ref[h * 80 : (h + 1) * 80, lanes] = o.astype(BF)
            att_send[block, h * 80 : (h + 1) * 80, :] = o.astype(BF)

        @pl.when(jnp.logical_and(mine, step == 7))
        def _():
            att_own.start()

        @pl.when(jnp.logical_not(jnp.logical_and(mine, step == 7)))
        def _():
            att_copy(block).start()

        for when, todo, m in WEIGHT_STEPS:

            @pl.when(step == when)
            def _(todo=todo, m=m):
                (weight_second if todo == 2 else weight_third)(m)

        return carry

    lax.fori_loop(0, 8, attend, 0)
    weight_second(2)
    lse_ref[2:8, :] = jnp.zeros((6, 2048), F32)

    def land(block, carry):
        @pl.when(jnp.logical_not(jnp.logical_and(mine, block == at.group)))
        def _():
            await_recv(att_ref.at[pl.ds(0, 160)], att_recv_sem.at[block])

        return carry

    @pl.when(mine)
    def _():
        att_own.wait()

    weight_last(0)
    lax.fori_loop(0, 8, land, 0)

    def across(left, right):
        return lax.dot_general(
            left, right, (((1,), (1,)), ((), ())), preferred_element_type=F32
        )

    x_load.wait()
    dy_load.wait()
    xf = x_mine[...].astype(F32)
    resid = xf + jnp.dot(jnp.transpose(att_ref[...]), weights[0], preferred_element_type=F32)
    inv = lax.rsqrt(jnp.mean(resid * resid, axis=1, keepdims=True) + EPS)
    normed_mlp = (resid * inv * mlp_gain).astype(BF)
    normed_mlp_ref[...] = jnp.transpose(normed_mlp)
    weight_last(1)
    up = jnp.dot(normed_mlp, weights[1], preferred_element_type=F32)
    sigma = 1.0 / (1.0 + jnp.exp(-up))
    act = (up * sigma).astype(BF)
    act_ref[...] = jnp.transpose(act)
    slope = sigma * (1.0 + up * (1.0 - sigma))
    weight_last(2)
    dy = dy_mine[...]
    up_grad = (across(dy, weights[2]) * slope).astype(BF)
    up_grad_ref[...] = up_grad
    scaled = across(up_grad, weights[1]) * mlp_gain
    resid_grad = dy.astype(F32) + inv * (
        scaled - resid * inv * inv * jnp.mean(scaled * resid, axis=1, keepdims=True)
    )
    resid_grad_ref[...] = resid_grad
    branch = resid_grad.astype(BF)
    branch_ref[...] = branch
    grad_ref[...] = across(weights[0], branch).astype(BF)
    result_ref[...] = resid + jnp.dot(act, weights[2], preferred_element_type=F32)

    w_save.wait()
    for k in range(8):
        rows = pl.ds(k * 256, 256)
        pltpu.make_async_copy(normed_ref.at[rows], normed_out.at[rows], save_sem.at[k, 0]).wait()
        pltpu.make_async_copy(qkv_ref.at[rows], qkv_out.at[rows], save_sem.at[k, 1]).wait()
    for copy in w_copies + aux_copies:
        copy.wait_send()
    pos_copy.wait_send()
    for m in range(3):
        for way in range(5) if SPLIT[m] else (0, 1, 3):
            weight_copy(m, way).wait_send()

    @pl.when(hub)
    def _():
        for k in range(8):
            for way, part in HUB_WAYS.get(k, ((0, 0), (0, 1), (1, 0), (1, 1), (2, 0), (2, 1))):
                await_recv(x_mine.at[halves[part]], x_send_sem.at[k, way, part])

    @pl.when(jnp.logical_not(hub))
    def _():
        x_far(0).wait_send()
        x_far(1).wait_send()

    def finish(block, carry):
        @pl.when(jnp.logical_not(jnp.logical_and(mine, block == c)))
        def _():
            att_copy(block).wait_send()

        return carry

    lax.fori_loop(0, 8, finish, 0)


def forward(*args):
    shape = jax.ShapeDtypeStruct
    dma = pltpu.SemaphoreType.DMA
    return pl.pallas_call(
        attend_kernel,
        name="forward",
        out_shape=(
            shape((1280, 256), BF),
            shape((2048, 1280), BF),
            shape((2048, 768), BF),
            shape((8, 2048), F32),
            shape((160, 2048), BF),
            shape((16, 1280), F32),
            shape((8, 2048), F32),
            shape((1280, 768), BF),
            shape((256, 1280), F32),
            shape((256, 1280), F32),
            shape((256, 1280), BF),
            shape((256, 1280), BF),
            shape((1280, 256), BF),
            shape((1280, 256), BF),
            shape((1280, 256), BF),
        ),
        in_specs=[pl.BlockSpec(memory_space=pltpu.SMEM)] + [ANY_SPEC] * 2 + [VMEM_SPEC] * 2 + [ANY_SPEC] * 4,
        out_specs=(VMEM_SPEC,) + (ANY_SPEC,) * 2 + (VMEM_SPEC,) * 4 + (ANY_SPEC,) + (VMEM_SPEC,) * 7,
        scratch_shapes=[
            pltpu.VMEM((256, 1280), BF),
            pltpu.VMEM((320, 3840), BF),
            pltpu.VMEM((256, 1280), BF),
            pltpu.VMEM((8, 256, 1280), BF),
            pltpu.VMEM((2048, 1280), BF),
            pltpu.VMEM((2048, 768), BF),
            pltpu.VMEM((1280, 768), BF),
            pltpu.VMEM((2, 320, 512), BF),
            pltpu.VMEM((1280, 512), BF),
            pltpu.VMEM((3, 1280, 1280), BF),
            pltpu.VMEM((4, 16, 384), BF),
            pltpu.VMEM((2, 8, 2048), F32),
            pltpu.VMEM((2, 128, 2048), BF),
            pltpu.VMEM((2048, LANES), F32),
            pltpu.VMEM((8, 160, 256), BF),
            dma((8, 3, 2)),
            dma((8, 2)),
            dma((4,)),
            dma((4,)),
            dma((4,)),
            dma((4,)),
            dma((2,)),
            dma((8,)),
            dma((8,)),
            dma((3, 5)),
            dma((3, 5)),
            dma((6,)),
            dma((8, 2)),
            dma((3,)),
        ],
        compiler_params=pltpu.CompilerParams(
            collective_id=0, has_side_effects=True, vmem_limit_bytes=VMEM_LIMIT
        ),
        cost_estimate=pl.CostEstimate(
            flops=20_000_000_000, bytes_accessed=40_000_000, transcendentals=8_400_000
        ),
    )(*args)


def add_into(target, source, rows, step):
    def one(k, carry):
        part = span(k * step, step, step)
        target[part, :] = (target[part, :].astype(F32) + source[part, :].astype(F32)).astype(BF)
        return carry

    lax.fori_loop(0, rows // step, one, 0)


def add_into(target, source, rows, step):
    def one(k, carry):
        part = span(k * step, step, step)
        target[part, :] = (target[part, :].astype(F32) + source[part, :].astype(F32)).astype(BF)
        return carry

    lax.fori_loop(0, rows // step, one, 0)


SUM_WAYS = ("xzyh", "xyzh", "zxyh")
SPREAD_WAYS = ("zhx", "hzx", "hxz")
HEAD_WAYS = "hzx"

PLAN = (
    "mt0", "mt1", "mt2", "prep", "m00", "m02", "take", "L00", "L01", "L02", "L03", "L04",
    "L05", "L06", "L07", "E0", "qs0", "m10", "m01", "L10", "L11", "L12", "L13", "L14", "L15",
    "qa0", "m12", "L16", "L17", "E1", "v0", "qs1", "nt0", "v1", "q00", "nt1", "nt2", "v2",
    "nt3", "na0", "m11", "na1", "v3", "qa1", "na2", "q10", "na3", "m20", "m22", "v4", "v5",
    "q01", "m21", "q20", "m30", "m32", "q11", "g00", "m31", "g02", "nb0", "nb1", "g10", "qc0",
    "g01", "g12", "q21", "qw0", "g22", "g11", "g20", "qc1", "nc_f", "nc_n", "qw1", "g21",
    "mw0", "mw2", "mw1", "nfin", "turn",
)

KEY_PARTS = 2
KEY_ROWS = 2048 // KEY_PARTS


def backward_kernel(
    grad_ref,
    att_hbm,
    branch_hbm,
    normed_mlp_hbm,
    up_grad_hbm,
    act_hbm,
    dy_hbm,
    qkv_hbm,
    lse_ref,
    out_hbm,
    place_ref,
    normed_hbm,
    w_hbm,
    mult_ref,
    x_hbm,
    resid_grad_hbm,
    gain_ref,
    first_out,
    second_out,
    third_out,
    slice_out,
    input_grad_ref,
    scale_ref,
    att_ref,
    branch_ref,
    normed_mlp_ref,
    up_grad_ref,
    act_ref,
    dy_ref,
    qkv_ref,
    out_ref,
    w_ref,
    x_ref,
    resid_grad_ref,
    grad_all,
    key_pos,
    k_turned,
    delta,
    key_sum,
    value_sum,
    turned,
    normed_part,
    n_core,
    n_x,
    n_z,
    n_last,
    sums,
    core_in,
    taken,
    slices,
    s1,
    s2,
    gathered,
    strip,
    scale_in,
    g_send_sem,
    g_recv_sem,
    local_sem,
    m_send,
    m_recv,
    q_send,
    q_recv,
    nc_send,
    nc_recv,
    n_send,
    n_recv,
    v_send,
    v_recv,
    load_sem,
):
    loads = {
        name: pltpu.make_async_copy(src, dst, load_sem.at[k])
        for k, (name, src, dst) in enumerate(
            (
                ("act", act_hbm, act_ref),
                ("dy", dy_hbm, dy_ref),
                ("normed", normed_mlp_hbm, normed_mlp_ref),
                ("up", up_grad_hbm, up_grad_ref),
                ("att", att_hbm, att_ref),
                ("branch", branch_hbm, branch_ref),
                ("qkv", qkv_hbm, qkv_ref),
                ("out", out_hbm, out_ref),
                ("w", w_hbm, w_ref),
                ("x", x_hbm, x_ref),
                ("resid", resid_grad_hbm, resid_grad_ref),
            )
        )
    }
    for load in loads.values():
        load.start()
    at = Place()
    meet_plane(at)
    c, f, core, half = at.c, at.f, at.core, at.half
    mine = core == half
    row = f // 2
    xbit, zbit = c % 2, (c // 2) % 2
    twin, across = dev(c, at.twin), dev(c, at.across)
    xpeer, zpeer, hpeer = dev(flip(c, 1), f), dev(flip(c, 2), f), dev(flip(c, 4), f)

    def remote(src, dst, send_sem, recv_sem, where):
        return pltpu.make_async_remote_copy(
            src_ref=src,
            dst_ref=dst,
            send_sem=send_sem,
            recv_sem=recv_sem,
            device_id=where,
            device_id_type=MESH,
        )

    def grad_copy(group, h):
        return remote(
            grad_ref.at[span(group * 160 + h * 80, 80, 80)],
            grad_all.at[h, pl.ds(0, 80), span(c * 256, 256, 256)],
            g_send_sem.at[group, h],
            g_recv_sem.at[c, h],
            dev(core * 4 + group // 2, at.plane + group % 2),
        )

    def grad_own(h):
        return pltpu.make_async_copy(
            grad_ref.at[span(at.group * 160 + h * 80, 80, 80)],
            grad_all.at[h, pl.ds(0, 80), span(c * 256, 256, 256)],
            local_sem.at[h],
        )

    def give(k, carry):
        group = flip(at.group, k)

        @pl.when(jnp.logical_and(mine, k == 0))
        def _():
            grad_own(0).start()
            grad_own(1).start()

        @pl.when(jnp.logical_not(jnp.logical_and(mine, k == 0)))
        def _():
            grad_copy(group, 0).start()
            grad_copy(group, 1).start()

        return carry

    lax.fori_loop(0, 8, give, 0)

    bits = {"y": row, "x": xbit, "z": zbit, "h": half}
    peers = {"y": across, "x": xpeer, "z": zpeer, "h": hpeer}
    results = (first_out, second_out, third_out)

    def finer(m):
        return "z" if SUM_WAYS[m].index("x") < SUM_WAYS[m].index("z") else "x"

    def cut(ref, way, bit):
        if way == "y":
            return (bit,)
        lead = (slice(None),) * (len(ref.shape) - 2)
        if way == "h":
            return lead + (slice(None), span(bit * 640, 640, 640))
        rows = ref.shape[-2] // 2
        return lead + (span(bit * rows, rows, rows),)

    def main_copy(stage, m):
        if stage < 0:
            y = stage + 2
            src, dst, to = sums.at[pl.ds((m * 2 + y) * 320, 320)], core_in.at[m, y], twin
        elif stage < 4:
            way = SUM_WAYS[m][stage]
            ref = core_in.at[m] if stage == 0 else taken[m][stage - 1]
            src, dst, to = ref.at[cut(ref, way, 1 - bits[way])], taken[m][stage], peers[way]
        else:
            way = SPREAD_WAYS[m][stage - 4]
            known = SPREAD_WAYS[m][: stage - 4]
            low = finer(m)
            high = "x" if low == "z" else "z"
            if high in known:
                rows = pl.ds(0, 320)
            elif low in known:
                rows = span(bits[high] * 160, 160, 160)
            else:
                rows = span(bits[high] * 160 + bits[low] * 80, 80, 80)
            lanes = pl.ds(0, 1280) if "h" in known else span(half * 640, 640, 640)
            src = dst = results[m].at[rows, lanes]
            to = peers[way]
        return remote(src, dst, m_send.at[stage + 2, m], m_recv.at[stage + 2, m], to)

    def added(ref, other, spot):
        for k in range(2) if len(ref.shape) == 3 else (None,):
            here = () if k is None else (k,)
            there = spot if k is None else (k,) + spot[1:]
            ref[here] = (ref[here].astype(F32) + other[there].astype(F32)).astype(BF)

    def main(stage, m):
        if stage == 0:
            for y in range(2):
                main_copy(y - 2, m).wait_recv()
                total = core_in[m, y].astype(F32) + weight_rows(m, 2 * y + core)
                core_in[m, y] = total.astype(BF)
        elif stage < 5:
            main_copy(stage - 1, m).wait_recv()
            way = SUM_WAYS[m][stage - 1]
            ref = core_in.at[m] if stage == 1 else taken[m][stage - 2]
            spot = cut(ref, way, bits[way])
            if stage < 4:
                added(taken[m][stage - 1], ref, spot)
            else:
                low = finer(m)
                high = "x" if low == "z" else "z"
                rows = span(bits[high] * 160 + bits[low] * 80, 80, 80)
                results[m][rows, span(half * 640, 640, 640)] = (
                    taken[m][3][...].astype(F32) + ref[spot].astype(F32)
                ).astype(BF)
        else:
            main_copy(stage - 1, m).wait_recv()
        if stage < 7:
            main_copy(stage, m).start()

    lefts = (act_ref, normed_mlp_ref, att_ref)
    rights = (dy_ref, up_grad_ref, branch_ref)

    def weight_rows(m, quarter):
        rows = span(quarter * 320, 320, 320)
        return jnp.dot(lefts[m][rows, :], rights[m][...], preferred_element_type=F32)

    def main_first(m):
        for name in (("act", "dy"), ("normed", "up"), ("att", "branch"))[m]:
            loads[name].wait()
        for y in range(2):
            part = weight_rows(m, 2 * y + 1 - core)
            sums[(m * 2 + y) * 320 : (m * 2 + y + 1) * 320, :] = part.astype(BF)
            main_copy(y - 2, m).start()

    def prepare():
        loads["qkv"].wait()
        for h in range(2):
            grad_all[h, 80:, :] = jnp.zeros((48, 2048), BF)
            k_turned[h] = jnp.transpose(qkv_ref[:, (2 + h) * LANES : (3 + h) * LANES])
        for k in range(8):
            block = place_ref[0:1, k * 256 : (k + 1) * 256]
            key_pos[k * 256 : (k + 1) * 256, :] = jnp.transpose(
                jnp.broadcast_to(block, (LANES, 256))
            )
        scale_ref[...] = jnp.zeros((8, LANES), F32)

    def take(k, carry):
        block = flip(c, k)

        @pl.when(jnp.logical_and(mine, k == 0))
        def _():
            grad_own(0).wait()
            grad_own(1).wait()

        @pl.when(jnp.logical_not(jnp.logical_and(mine, k == 0)))
        def _():
            for h in range(2):
                await_recv(
                    grad_all.at[h, pl.ds(0, 80), pl.ds(0, 256)], g_recv_sem.at[block, h]
                )

        return carry

    def take_all():
        loads["out"].wait()
        lax.fori_loop(0, 8, take, 0)
        for h in range(2):
            delta[h : h + 1, :] = jnp.sum(
                grad_all[h, :80, :].astype(F32) * out_ref[h * 80 : (h + 1) * 80, :].astype(F32),
                axis=0,
                keepdims=True,
            )

    def head_copy(stage, h):
        if stage == 0:
            src, dst, to = slices.at[h, :, span((1 - row) * 640, 640, 640)], s1.at[h], across
        elif stage == 1:
            src, dst, to = s1.at[h, span(128 - half * 128, 128, 128)], s2.at[h], hpeer
        elif stage < 5:
            way = HEAD_WAYS[stage - 2]
            known = HEAD_WAYS[: stage - 2]
            where = (core,) + tuple(slice(None) if d in known else bits[d] for d in "xz") + (h,)
            rows = slice(None) if "h" in known else span(half * 128, 128, 128)
            src = dst = gathered.at[where + (rows,)]
            to = peers[way]
        else:
            src = dst = gathered.at[core, :, :, h]
            to = twin
        return remote(src, dst, q_send.at[stage, h], q_recv.at[stage, h], to)

    def head(stage, h):
        if stage > 0:
            head_copy(stage - 1, h).wait_recv()
        if stage == 1:
            add_into(s1.at[h], slices.at[h, :, span(row * 640, 640, 640)], 256, 128)
        if stage == 2:
            own = span(half * 128, 128, 128)
            gathered[core, xbit, zbit, h, own, :] = (
                s2[h].astype(F32) + s1[h, own, :].astype(F32)
            ).astype(BF)
        if stage < 6:
            head_copy(stage, h).start()

    def normed_load(part):
        return pltpu.make_async_copy(
            normed_hbm.at[:, pl.ds(part * 256, 256)], normed_part.at[part % 2], local_sem.at[2 + part % 2]
        )

    def attend_head(h, hooks):
        key_sum[...] = jnp.zeros((2048, LANES), F32)
        value_sum[...] = jnp.zeros((2048, LANES), F32)

        def block_grad(block, carry):
            lanes = span(block * 256, 256, 256)
            high = place_ref[0:1, lanes]
            least = place_ref[1:2, lanes]
            query = qkv_ref[lanes, h * LANES : (h + 1) * LANES]
            grad_t = grad_all[h, :, lanes]
            q_grad = jnp.zeros((LANES, 256), F32)
            for part in range(KEY_PARTS):
                some = slice(part * KEY_ROWS, (part + 1) * KEY_ROWS)
                kp = key_pos[some, :]
                kp = jnp.concatenate([kp, kp], axis=1)
                keys = qkv_ref[some, (2 + h) * LANES : (3 + h) * LANES]
                values = qkv_ref[some, (4 + h) * LANES : (5 + h) * LANES]
                s = lax.dot_general(
                    keys, query, (((1,), (1,)), ((), ())), preferred_element_type=F32
                )
                visible = (kp >= least) & (kp <= high)
                p = jnp.exp(jnp.where(visible, s - lse_ref[h : h + 1, lanes], FLOOR))
                gp = jnp.dot(values, grad_t, preferred_element_type=F32)
                gs = (p * (gp - delta[h : h + 1, lanes])).astype(BF)
                value_sum[some, :] += lax.dot_general(
                    p.astype(BF), grad_t, (((1,), (1,)), ((), ())), preferred_element_type=F32
                )
                key_sum[some, :] += jnp.dot(gs, query, preferred_element_type=F32)
                q_grad += jnp.dot(k_turned[h, :, some], gs, preferred_element_type=F32)
            scale_ref[0:1, :] += jnp.sum(
                jnp.transpose(q_grad) * query.astype(F32), axis=0, keepdims=True
            )
            turned[h * LANES : (h + 1) * LANES, lanes] = (q_grad * mult_ref[:, 0:1]).astype(BF)
            for step, todo in hooks.items():

                @pl.when(block == step)
                def _(todo=todo):
                    for one in todo:
                        one()

            return carry

        lax.fori_loop(0, 8, block_grad, 0)

    def attend_end(h):
        for j, total in ((1, key_sum), (2, value_sum)):
            low = jnp.transpose(total[...]).astype(BF)
            turned[(2 * j + h) * LANES : (2 * j + h + 1) * LANES, :] = low

    def head_first(h):
        slices[h, 240:, :] = jnp.zeros((16, 1280), BF)
        for part in range(5):
            normed_load(part).wait()
            if part + 1 < 5:
                normed_load(part + 1).start()
            for j in range(3):
                first = (2 * j + h) * LANES
                slices[h, j * 80 : (j + 1) * 80, part * 256 : (part + 1) * 256] = jnp.dot(
                    turned[first : first + 80, :],
                    normed_part[part % 2],
                    preferred_element_type=F32,
                ).astype(BF)
        if h == 0:
            normed_load(0).start()
        head(0, h)

    def norm_bits(k):
        return (1 - xbit, 1 - xbit, xbit, xbit)[k], (1 - zbit, zbit, 1 - zbit, zbit)[k]

    def norm_spot(k, hh):
        slot = 2 * k + hh
        return sums.at[pl.ds(slot // 5 * 640, 640), pl.ds(slot % 5 * 256, 256)]

    def norm_copy(stage, k, hh=0):
        if stage == 0:
            return remote(
                norm_spot(k, hh), n_core.at[k, hh], nc_send.at[k, hh], nc_recv.at[k, hh], twin
            )
        took = k
        if stage == 1:
            ends = n_core.at[k], n_x.at[k], xpeer
        elif stage == 2:
            ends = n_core.at[2, (1 - half, half)[k]], n_z.at[k], zpeer
        else:
            to = dev(flip(c, 4), at.pack) if k == 0 else dev(c, at.twin)
            took = (core, 2)[k]
            ends = n_core.at[3, (1 - half, half)[k]], n_last.at[core], to
        return remote(ends[0], ends[1], n_send.at[stage, k], n_recv.at[stage, took], ends[2])

    def norm_part(k, hh, which):
        xs, zs = norm_bits(k)
        lanes = span((hh * 4 + zs * 2 + xs) * 256, 256, 256)
        rows = span(which * 640, 640, 640)
        return jnp.dot(w_ref[rows, :], turned[:, lanes], preferred_element_type=F32)

    def norm_first(k):
        if k == 0:
            loads["w"].wait()
            for m in range(3):
                for stage in range(2):
                    main_copy(stage - 2, m).wait_send()
        for hh in range(2):
            norm_spot(k, hh)[...] = norm_part(k, hh, 1 - core).astype(BF)
            norm_copy(0, k, hh).start()

    def norm_core(k):
        for hh in range(2):
            norm_copy(0, k, hh).wait_recv()
            n_core[k, hh] = (n_core[k, hh].astype(F32) + norm_part(k, hh, core)).astype(BF)
        if k < 2:
            norm_copy(1, k).start()

    def scale_copy(stage):
        where = (twin, across, xpeer, zpeer, hpeer)[stage]
        return remote(scale_ref, scale_in.at[stage], v_send.at[stage], v_recv.at[stage], where)

    def tiny(stage):
        if stage > 0:
            scale_copy(stage - 1).wait()
            scale_ref[...] += scale_in[stage - 1]
        if stage < 5:
            scale_copy(stage).start()

    def norm_x(k):
        norm_copy(1, k).wait_recv()
        for hh in range(2):
            add_into(n_core.at[2 + k, hh], n_x.at[k, hh], 640, 80)
        if k == 0:
            norm_copy(2, 0).start()
            norm_copy(2, 1).start()

    def norm_far():
        norm_copy(2, 0).wait_recv()
        add_into(n_core.at[3, 1 - half], n_z.at[0], 640, 80)
        norm_copy(3, 0).start()

    def norm_near():
        norm_copy(2, 1).wait_recv()
        add_into(n_core.at[3, half], n_z.at[1], 640, 80)

        @pl.when(jnp.logical_not(mine))
        def _():
            norm_copy(3, 1).start()

    def norm_last():
        loads["x"].wait()
        loads["resid"].wait()
        @pl.when(mine)
        def _():
            n_last[core] = n_core[3, half]
            await_recv(n_last.at[0], n_recv.at[3, 2])

        @pl.when(jnp.logical_not(mine))
        def _():
            await_recv(n_last.at[0], n_recv.at[3, 0])
            await_recv(n_last.at[1], n_recv.at[3, 1])

        xf = x_ref[...].astype(F32)
        inv = lax.rsqrt(jnp.mean(xf * xf, axis=1, keepdims=True) + EPS)
        scaled = jnp.concatenate(
            [jnp.transpose(n_last[k].astype(F32)) for k in range(2)], axis=1
        ) * gain_ref[0:1, :]
        input_grad_ref[...] = resid_grad_ref[...] + inv * (
            scaled - xf * inv * inv * jnp.mean(scaled * xf, axis=1, keepdims=True)
        )

    def turn_all():
        for k in range(4):
            for hh in range(2):
                norm_copy(0, k, hh).wait_send()
        for core_k in range(2):
            for m4 in range(4):
                group = 2 * m4 + core_k
                for h in range(2):
                    for j in range(3):
                        start = j * 1280 + (group * 2 + h) * 80
                        sums[
                            start % 1920 : start % 1920 + 80, start // 1920 * 640 : start // 1920 * 640 + 640
                        ] = gathered[core_k, m4 % 2, m4 // 2, h, j * 80 : (j + 1) * 80, :]

        for part in range(2):

            def turn(k, carry, part=part):
                strip[...] = jnp.transpose(sums[span(k * LANES, LANES, LANES), part * 640 : part * 640 + 640])
                slice_out[:, span(part * 1920 + k * LANES, LANES, LANES)] = strip[span(core * 320, 320, 320), :]
                return carry

            lax.fori_loop(0, 15, turn, 0)


    tasks = {"prep": prepare, "take": take_all, "nb0": lambda: norm_x(0), "nb1": lambda: norm_x(1)}
    tasks |= {"nc_f": norm_far, "nc_n": norm_near, "nfin": norm_last, "turn": turn_all}
    for m in range(3):
        tasks[f"mt{m}"] = functools.partial(main_first, m)
        for stage in range(4):
            tasks[f"m{stage}{m}"] = functools.partial(main, stage, m)
        for stage in range(3):
            tasks[f"g{stage}{m}"] = functools.partial(main, 4 + stage, m)
        tasks[f"mw{m}"] = functools.partial(main, 7, m)
    for h in range(2):
        tasks[f"E{h}"] = functools.partial(attend_end, h)
        tasks[f"qs{h}"] = functools.partial(head_first, h)
        for stage, name in enumerate(("qa", "q0", "q1", "q2", "qc", "qw")):
            tasks[f"{name}{h}"] = functools.partial(head, 1 + stage, h)
    for k in range(4):
        tasks[f"nt{k}"] = functools.partial(norm_first, k)
        tasks[f"na{k}"] = functools.partial(norm_core, k)
    for stage in range(6):
        tasks[f"v{stage}"] = functools.partial(tiny, stage)

    normed_load(0).start()
    spot = 0
    while spot < len(PLAN):
        name = PLAN[spot]
        if name[0] != "L":
            tasks[name]()
            spot += 1
            continue
        h, step, hooks = int(name[1]), -1, {}
        while step < 7 or PLAN[spot][0] == "L":
            if PLAN[spot][0] == "L":
                step = int(PLAN[spot][2])
                if step == 7:
                    spot += 1
                    break
            else:
                hooks.setdefault(step, []).append(tasks[PLAN[spot]])
            spot += 1
        attend_head(h, hooks)

    def sent(block, carry):
        own_in = jnp.logical_and(mine, block == at.group)

        @pl.when(jnp.logical_not(own_in))
        def _():
            for h in range(2):
                grad_copy(block, h).wait_send()

        return carry

    lax.fori_loop(0, 8, sent, 0)
    for m in range(3):
        for stage in range(7):
            main_copy(stage, m).wait_send()
    for h in range(2):
        for stage in range(6):
            head_copy(stage, h).wait_send()
    for k in range(2):
        norm_copy(1, k).wait_send()
        norm_copy(2, k).wait_send()
    norm_copy(3, 0).wait_send()

    @pl.when(jnp.logical_not(mine))
    def _():
        norm_copy(3, 1).wait_send()


def sum_slots():
    slots = []
    for ways in SUM_WAYS:
        shape, own = [2, 320, 1280], []
        for way in ways:
            if way == "y":
                shape = shape[1:]
            else:
                shape[-1 if way == "h" else -2] //= 2
            own.append(pltpu.VMEM(tuple(shape), BF))
        slots.append(own)
    return slots


def backward(*args):
    shape = jax.ShapeDtypeStruct
    dma = pltpu.SemaphoreType.DMA
    specs = [ANY_SPEC] * 17
    for k in (8, 10, 13, 16):
        specs[k] = VMEM_SPEC
    return pl.pallas_call(
        backward_kernel,
        name="backward",
        out_shape=(
            shape((320, 1280), BF),
            shape((320, 1280), BF),
            shape((320, 1280), BF),
            shape((320, 3840), BF),
            shape((256, 1280), F32),
            shape((8, LANES), F32),
        ),
        in_specs=specs,
        out_specs=(VMEM_SPEC,) * 6,
        scratch_shapes=[
            pltpu.VMEM((1280, 256), BF),
            pltpu.VMEM((256, 1280), BF),
            pltpu.VMEM((1280, 256), BF),
            pltpu.VMEM((256, 1280), BF),
            pltpu.VMEM((1280, 256), BF),
            pltpu.VMEM((256, 1280), BF),
            pltpu.VMEM((2048, 768), BF),
            pltpu.VMEM((160, 2048), BF),
            pltpu.VMEM((1280, 768), BF),
            pltpu.VMEM((256, 1280), BF),
            pltpu.VMEM((256, 1280), F32),
            pltpu.VMEM((2, 128, 2048), BF),
            pltpu.VMEM((2048, LANES), F32),
            pltpu.VMEM((2, 128, 2048), BF),
            pltpu.VMEM((8, 2048), F32),
            pltpu.VMEM((2048, LANES), F32),
            pltpu.VMEM((2048, LANES), F32),
            pltpu.VMEM((768, 2048), BF),
            pltpu.VMEM((2, 2048, 256), BF),
            pltpu.VMEM((4, 2, 640, 256), BF),
            pltpu.VMEM((2, 2, 640, 256), BF),
            pltpu.VMEM((2, 640, 256), BF),
            pltpu.VMEM((2, 640, 256), BF),
            pltpu.VMEM((1920, 1280), BF),
            pltpu.VMEM((3, 2, 320, 1280), BF),
            sum_slots(),
            pltpu.VMEM((2, 256, 1280), BF),
            pltpu.VMEM((2, 256, 640), BF),
            pltpu.VMEM((2, 128, 640), BF),
            pltpu.VMEM((2, 2, 2, 2, 256, 640), BF),
            pltpu.VMEM((640, LANES), BF),
            pltpu.VMEM((5, 8, LANES), F32),
            dma((8, 2)),
            dma((8, 2)),
            dma((4,)),
            dma((9, 3)),
            dma((9, 3)),
            dma((6, 2)),
            dma((6, 2)),
            dma((4, 2)),
            dma((4, 2)),
            dma((4, 4)),
            dma((4, 4)),
            dma((5,)),
            dma((5,)),
            dma((11,)),
        ],
        compiler_params=pltpu.CompilerParams(
            collective_id=1, has_side_effects=True, vmem_limit_bytes=VMEM_LIMIT
        ),
        cost_estimate=pl.CostEstimate(
            flops=30_000_000_000, bytes_accessed=60_000_000, transcendentals=8_400_000
        ),
    )(*args)


def fast_body(
    tokens,
    lengths,
    position,
    qkv_weight,
    out_weight,
    up_weight,
    down_weight,
    attn_gain,
    mlp_gain,
    query_scale,
    cotangent,
):
    f = lax.axis_index("fsdp")
    x, dy = tokens[0], cotangent[0]
    small = [jnp.pad(a, (0, 384 - a.shape[0])) for a in (attn_gain, mlp_gain, query_scale)]
    small = jnp.stack(small + [jnp.zeros((384,), BF)] * 13)
    (
        att_t, normed, qkv, lse, out, auxsum, place, w_heads,
        result, resid_grad, branch_grad, up_grad, act_t, normed_mlp_t, grad_t,
    ) = forward(
        lengths, x, qkv_weight, small, position, out_weight, up_weight, down_weight, dy
    )
    scale_float = auxsum[2, :80]
    base_scale = LOG2E / math.sqrt(80)
    soft = jax.nn.softplus(scale_float)
    mult = jnp.broadcast_to(jnp.pad(base_scale * soft, (0, 48))[:, None], (LANES, LANES))
    g_down, g_up, g_out, g_qkv, input_grad, scale_sum = backward(
        grad_t,
        att_t,
        branch_grad,
        normed_mlp_t,
        up_grad,
        act_t,
        dy,
        qkv,
        lse,
        out,
        place,
        normed,
        w_heads,
        mult,
        x,
        resid_grad,
        auxsum,
    )
    g_down, g_up, g_out = (g.astype(F32) for g in (g_down, g_up, g_out))
    g_qkv = g_qkv.astype(F32)
    grad_attn_gain = jnp.sum(qkv_weight.astype(F32) * g_qkv, axis=1) / attn_gain.astype(F32)
    grad_mlp_gain = jnp.sum(up_weight.astype(F32) * g_up, axis=1) / mlp_gain.astype(F32)
    grad_scale = scale_sum[0, :80] / soft * jax.nn.sigmoid(scale_float)
    return (
        result[None],
        input_grad[None],
        g_qkv,
        g_out,
        g_up,
        g_down,
        grad_attn_gain,
        grad_mlp_gain,
        lax.dynamic_slice_in_dim(grad_scale, f * 20, 20),
    )


def solution(mesh):
    placed = (
        P("fsdp", "ctx", None),
        P("fsdp", None),
        P("fsdp", None),
        P("fsdp", None),
        P("fsdp", None),
        P("fsdp", None),
        P("fsdp", None),
        P("fsdp"),
        P("fsdp"),
        P("fsdp"),
        P("fsdp", "ctx", None),
    )
    fits = mesh.shape["ctx"] == 8 and mesh.shape["fsdp"] == 4
    return jax.shard_map(
        fast_body if fits else body,
        mesh=mesh,
        in_specs=placed,
        out_specs=(
            P("fsdp", "ctx", None),
            P("fsdp", "ctx", None),
            P("fsdp", None),
            P("fsdp", None),
            P("fsdp", None),
            P("fsdp", None),
            P("fsdp"),
            P("fsdp"),
            P("fsdp"),
        ),
        check_vma=False,
    )
```

profile of v0, /device:TPU:0, one launch (start us, length us, event | category | flops | bytes accessed | tf_op | source)
XLA Modules:
  0.0 275.3 jit_solution(4495624998563888485)
XLA Ops:
  0.6 0.7 pad.15
  1.3 0.7 pad.16
  2.0 0.7 pad.17
  2.7 1.2 stack.23.aux_ref
  3.9 85.5 %forward.1 = (bf16[1280,256]{1,0:T(8,128)(2,1)}, bf16[2048,1280]{1,0:T(8,128)(2,1)}, bf16[2048,768]{1,0:T(8,128)(2,1)}, f32[8,2048]{1,0:T(8,128)}, bf16[160,2048...) custom-call(s32[1,4]{1,0:T(1,128)} %ends_ref.1, ...), custom_call_target="tpu_custom_call" | custom-call | flops 20000000000 | bytes 40000000 | tf_op jit(solution)/shard_map/forward/pallas_call | solution.py:884
  89.4 0.7 broadcast_multiply_fusion
  90.1 0.7 broadcast_in_dim.13.mult_ref
  90.9 0.0 copy-start
  90.9 170.7 %backward.1 = (bf16[320,1280]{1,0:T(8,128)(2,1)}, bf16[320,1280]{1,0:T(8,128)(2,1)}, bf16[320,1280]{1,0:T(8,128)(2,1)}, bf16[320,3840]{1,0:T(8,128)(2,1)}, f32[256,1280]{1,0:T(8,128)}, /*index=5*/f32[8,128]{1,0:T(8,128)}) custom-call(bf16[1280,256]{1,0:T(8,128)(2,1)} %get-tuple-element.31.grad_ref, bf16[1280,256]{1,0:T(8,128)(2,1)} %get-tuple-element.32.att_hbm, ...), custom_call_target="tpu_custom_call" | custom-call | flops 30000001024 | bytes 60000000 | tf_op jit(solution)/shard_map/backward/pallas_call | solution.py:1562
  261.6 0.0 copy-done
  261.6 0.0 copy-start.6
  261.6 4.6 %multiply_reduce_fusion = (f32[320]{0:T(512)S(1)}, f32[320,3840]{1,0:T(8,128)}) fusion(bf16[320,3840]{1,0:T(8,128)(2,1)S(1)} %copy-done, bf16[320,3840]{1,0:T(8,128)(2,1)} %get-tuple-element.46), kind=kLoop, calls=%fused_computation | loop fusion | flops 4914880 | bytes 9831680 | tf_op jit(solution)/shard_map/reduce_sum | solution.py:1680
  266.2 0.0 copy-start.3
  266.2 0.0 copy-start.5
  266.2 0.0 copy-done.6
  266.2 1.3 convert_element_type.32
  267.5 0.0 copy-start.4
  267.5 0.1 copy-done.3
  267.7 0.6 copy-done.5
  268.2 1.4 multiply_reduce_fusion.1
  269.6 0.0 copy-done.4
  269.6 0.0 copy-start.2
  269.6 1.3 convert_element_type.34
  270.9 0.0 copy-done.7
  270.9 0.0 copy-done.8
  270.9 0.6 convert_divide_fusion
  271.5 0.7 divide_multiply_fusion
  272.2 0.6 dynamic_slice.3
  272.8 0.0 copy-done.1
  272.8 1.1 copy.22
  273.8 0.0 copy-done.2
  273.8 1.1 copy.23
  (10 shorter events, 0.0 us)
Async XLA Ops:
  90.9 170.7 %copy-start = (bf16[320,3840]{1,0:T(8,128)(2,1)S(1)}, bf16[320,3840]{1,0:T(8,128)(2,1)}, u32[]{:S(2)}) copy-start(bf16[320,3840]{1,0:T(8,128)(2,1)} %w_ref.1) | copy-start | bytes 7372804
  261.6 4.7 %copy-start.6 = (bf16[320,1280]{1,0:T(8,128)(2,1)S(1)}, bf16[320,1280]{1,0:T(8,128)(2,1)}, u32[]{:S(2)}) copy-start(bf16[320,1280]{1,0:T(8,128)(2,1)} %get-tuple-element.47) | copy-start | bytes 2457604
  266.2 1.4 copy-start.3
  266.2 2.0 copy-start.5
  267.5 2.1 copy-start.4
  269.6 1.3 copy-start.7
  269.6 1.3 copy-start.8
  269.6 3.2 %copy-start.1 = (f32[256,1280]{1,0:T(8,128)S(1)}, f32[256,1280]{1,0:T(8,128)}, u32[]{:S(2)}) copy-start(f32[256,1280]{1,0:T(8,128)} %get-tuple-element.30) | copy-start | bytes 3932164
  269.6 4.2 %copy-start.2 = (f32[256,1280]{1,0:T(8,128)S(1)}, f32[256,1280]{1,0:T(8,128)}, u32[]{:S(2)}) copy-start(f32[256,1280]{1,0:T(8,128)} %get-tuple-element.45) | copy-start | bytes 3932164
where the time goes:
time: 279 us; the launch traced here: 275 us
  Pallas kernels  256 us (92%)
  other arithmetic  10.5 us (4%)
  local copies, waits for them, and re-layouts  7.44 us (3%)
    pallas_call x1, Pallas kernels, backward(): pl.pallas_call(backward_kernel, name='backward', out_shape=(shape((320, 1...  171 us
    pallas_call x1, Pallas kernels, forward(): pl.pallas_call(attend_kernel, name='forward', out_shape=(shape((1280, 256...  85.5 us

commit v1 on v0

--- a/solution.py
+++ b/solution.py
@@ -952,27 +952,18 @@
     lax.fori_loop(0, rows // step, one, 0)
 
 
-def add_into(target, source, rows, step):
-    def one(k, carry):
-        part = span(k * step, step, step)
-        target[part, :] = (target[part, :].astype(F32) + source[part, :].astype(F32)).astype(BF)
-        return carry
-
-    lax.fori_loop(0, rows // step, one, 0)
-
-
-SUM_WAYS = ("xzyh", "xyzh", "zxyh")
-SPREAD_WAYS = ("zhx", "hzx", "hxz")
+SUM_WAYS = ("yxzh", "zyxh", "zxyh")
+SPREAD_WAYS = ("zhx", "hxz", "hxz")
 HEAD_WAYS = "hzx"
 
 PLAN = (
-    "mt0", "mt1", "mt2", "prep", "m00", "m02", "take", "L00", "L01", "L02", "L03", "L04",
-    "L05", "L06", "L07", "E0", "qs0", "m10", "m01", "L10", "L11", "L12", "L13", "L14", "L15",
-    "qa0", "m12", "L16", "L17", "E1", "v0", "qs1", "nt0", "v1", "q00", "nt1", "nt2", "v2",
-    "nt3", "na0", "m11", "na1", "v3", "qa1", "na2", "q10", "na3", "m20", "m22", "v4", "v5",
-    "q01", "m21", "q20", "m30", "m32", "q11", "g00", "m31", "g02", "nb0", "nb1", "g10", "qc0",
-    "g01", "g12", "q21", "qw0", "g22", "g11", "g20", "qc1", "nc_f", "nc_n", "qw1", "g21",
-    "mw0", "mw2", "mw1", "nfin", "turn",
+    "prep", "mt0", "m00", "mt2", "m02", "mt1", "take", "L00", "L01", "L02", "L03", "L04",
+    "m01", "L05", "L06", "L07", "E0", "qs0", "L10", "L11", "L12", "L13", "L14", "L15", "L16",
+    "qa0", "m10", "L17", "m12", "E1", "v0", "qs1", "nt0", "nt1", "nt2", "q00", "v1", "nt3",
+    "v2", "v3", "na0", "v4", "na1", "na2", "qa1", "na3", "v5", "m11", "q10", "m20", "q01",
+    "m22", "m21", "m32", "m30", "q11", "q20", "g02", "g00", "m31", "g12", "nb0", "g10", "g01",
+    "nb1", "q21", "g22", "g11", "g20", "nc_f", "nc_n", "g21", "qc0", "qw0", "mw2", "qc1",
+    "mw0", "nfin", "qw1", "mw1", "turn",
 )
 
 KEY_PARTS = 2
@@ -1001,8 +992,13 @@
     second_out,
     third_out,
     slice_out,
-    input_grad_ref,
+    input_grad_out,
     scale_ref,
+    first_ref,
+    second_ref,
+    third_ref,
+    slice_ref,
+    input_ref,
     att_ref,
     branch_ref,
     normed_mlp_ref,
@@ -1033,7 +1029,6 @@
     s1,
     s2,
     gathered,
-    strip,
     scale_in,
     g_send_sem,
     g_recv_sem,
@@ -1049,6 +1044,7 @@
     v_send,
     v_recv,
     load_sem,
+    save_sem,
 ):
     loads = {
         name: pltpu.make_async_copy(src, dst, load_sem.at[k])
@@ -1124,7 +1120,7 @@
 
     bits = {"y": row, "x": xbit, "z": zbit, "h": half}
     peers = {"y": across, "x": xpeer, "z": zpeer, "h": hpeer}
-    results = (first_out, second_out, third_out)
+    results = (first_ref, second_ref, third_ref)
 
     def finer(m):
         return "z" if SUM_WAYS[m].index("x") < SUM_WAYS[m].index("z") else "x"
@@ -1192,6 +1188,8 @@
             main_copy(stage - 1, m).wait_recv()
         if stage < 7:
             main_copy(stage, m).start()
+        else:
+            save(m).start()
 
     lefts = (act_ref, normed_mlp_ref, att_ref)
     rights = (dy_ref, up_grad_ref, branch_ref)
@@ -1276,6 +1274,8 @@
             ).astype(BF)
         if stage < 6:
             head_copy(stage, h).start()
+        else:
+            head_flat(h)
 
     def normed_load(part):
         return pltpu.make_async_copy(
@@ -1444,33 +1444,57 @@
         scaled = jnp.concatenate(
             [jnp.transpose(n_last[k].astype(F32)) for k in range(2)], axis=1
         ) * gain_ref[0:1, :]
-        input_grad_ref[...] = resid_grad_ref[...] + inv * (
+        input_ref[...] = resid_grad_ref[...] + inv * (
             scaled - xf * inv * inv * jnp.mean(scaled * xf, axis=1, keepdims=True)
         )
-
-    def turn_all():
-        for k in range(4):
-            for hh in range(2):
-                norm_copy(0, k, hh).wait_send()
+        save(3).start()
+
+    def head_flat(h):
+        if h == 0:
+            for k in range(4):
+                for hh in range(2):
+                    norm_copy(0, k, hh).wait_send()
         for core_k in range(2):
             for m4 in range(4):
-                group = 2 * m4 + core_k
-                for h in range(2):
-                    for j in range(3):
-                        start = j * 1280 + (group * 2 + h) * 80
-                        sums[
-                            start % 1920 : start % 1920 + 80, start // 1920 * 640 : start // 1920 * 640 + 640
-                        ] = gathered[core_k, m4 % 2, m4 // 2, h, j * 80 : (j + 1) * 80, :]
-
+                for j in range(3):
+                    start = j * 1280 + (4 * m4 + 2 * core_k + h) * 80
+                    first = start // 1920 * 640
+                    sums[start % 1920 : start % 1920 + 80, first : first + 640] = gathered[
+                        core_k, m4 % 2, m4 // 2, h, j * 80 : (j + 1) * 80, :
+                    ]
+
+    def save(k):
+        src, dst = (
+            (first_ref, first_out),
+            (second_ref, second_out),
+            (third_ref, third_out),
+            (input_ref, input_grad_out),
+            (slice_ref.at[:, pl.ds(0, 1920)], slice_out.at[:, pl.ds(0, 1920)]),
+            (slice_ref.at[:, pl.ds(1920, 1920)], slice_out.at[:, pl.ds(1920, 1920)]),
+        )[k]
+        return pltpu.make_async_copy(src, dst, save_sem.at[k])
+
+    def turn_all():
         for part in range(2):
 
             def turn(k, carry, part=part):
-                strip[...] = jnp.transpose(sums[span(k * LANES, LANES, LANES), part * 640 : part * 640 + 640])
-                slice_out[:, span(part * 1920 + k * LANES, LANES, LANES)] = strip[span(core * 320, 320, 320), :]
+                rows = span(k * 384, 384, 384)
+                lanes = span(part * 1920 + k * 384, 384, 384)
+
+                @pl.when(core == 0)
+                def _():
+                    strip = jnp.transpose(sums[rows, part * 640 : part * 640 + 384])
+                    slice_ref[:, lanes] = strip[:320]
+
+                @pl.when(core == 1)
+                def _():
+                    strip = jnp.transpose(sums[rows, part * 640 + 256 : part * 640 + 640])
+                    slice_ref[:, lanes] = strip[64:]
+
                 return carry
 
-            lax.fori_loop(0, 15, turn, 0)
-
+            lax.fori_loop(0, 5, turn, 0)
+            save(4 + part).start()
 
     tasks = {"prep": prepare, "take": take_all, "nb0": lambda: norm_x(0), "nb1": lambda: norm_x(1)}
     tasks |= {"nc_f": norm_far, "nc_n": norm_near, "nfin": norm_last, "turn": turn_all}
@@ -1512,6 +1536,8 @@
             spot += 1
         attend_head(h, hooks)
 
+    for k in range(6):
+        save(k).wait()
     def sent(block, carry):
         own_in = jnp.logical_and(mine, block == at.group)
 
@@ -1571,8 +1597,13 @@
             shape((8, LANES), F32),
         ),
         in_specs=specs,
-        out_specs=(VMEM_SPEC,) * 6,
+        out_specs=(ANY_SPEC,) * 5 + (VMEM_SPEC,),
         scratch_shapes=[
+            pltpu.VMEM((320, 1280), BF),
+            pltpu.VMEM((320, 1280), BF),
+            pltpu.VMEM((320, 1280), BF),
+            pltpu.VMEM((320, 3840), BF),
+            pltpu.VMEM((256, 1280), F32),
             pltpu.VMEM((1280, 256), BF),
             pltpu.VMEM((256, 1280), BF),
             pltpu.VMEM((1280, 256), BF),
@@ -1603,7 +1634,6 @@
             pltpu.VMEM((2, 256, 640), BF),
             pltpu.VMEM((2, 128, 640), BF),
             pltpu.VMEM((2, 2, 2, 2, 256, 640), BF),
-            pltpu.VMEM((640, LANES), BF),
             pltpu.VMEM((5, 8, LANES), F32),
             dma((8, 2)),
             dma((8, 2)),
@@ -1619,6 +1649,7 @@
             dma((5,)),
             dma((5,)),
             dma((11,)),
+            dma((6,)),
         ],
         compiler_params=pltpu.CompilerParams(
             collective_id=1, has_side_effects=True, vmem_limit_bytes=VMEM_LIMIT

time: 279 us -> 270 us (0.968)
  Pallas kernels: 256 us -> 248 us
    pallas_call x1, Pallas kernels: 171 us -> 163 us  [backward(): pl.pallas_call(backward_kernel, name='backward', out_shape=(shape((320, 1...]
where the time goes in v1:
time: 270 us; the launch traced here: 267 us
  Pallas kernels  248 us (92%)
  other arithmetic  10.5 us (4%)
  local copies, waits for them, and re-layouts  7.44 us (3%)
    pallas_call x1, Pallas kernels, backward(): pl.pallas_call(backward_kernel, name='backward', out_shape=(shape((320, 1...  163 us
    pallas_call x1, Pallas kernels, forward(): pl.pallas_call(attend_kernel, name='forward', out_shape=(shape((1280, 256...  85.5 us

profile of v1, /device:TPU:0, one launch (start us, length us, event | category | flops | bytes accessed | tf_op | source)
XLA Modules:
  0.0 267.1 jit_solution(7008612198635838493)
XLA Ops:
  0.6 0.7 pad.15
  1.3 0.7 pad.16
  2.0 0.7 pad.17
  2.7 1.2 stack.23.aux_ref
  3.9 85.5 %forward.1 = (bf16[1280,256]{1,0:T(8,128)(2,1)}, bf16[2048,1280]{1,0:T(8,128)(2,1)}, bf16[2048,768]{1,0:T(8,128)(2,1)}, f32[8,2048]{1,0:T(8,128)}, bf16[160,2048...) custom-call(s32[1,4]{1,0:T(1,128)} %ends_ref.1, ...), custom_call_target="tpu_custom_call" | custom-call | flops 20000000000 | bytes 40000000 | tf_op jit(solution)/shard_map/forward/pallas_call | solution.py:884
  89.4 0.7 broadcast_multiply_fusion
  90.1 0.7 broadcast_in_dim.13.mult_ref
  90.9 0.0 copy-start
  90.9 162.5 %backward.1 = (bf16[320,1280]{1,0:T(8,128)(2,1)}, bf16[320,1280]{1,0:T(8,128)(2,1)}, bf16[320,1280]{1,0:T(8,128)(2,1)}, bf16[320,3840]{1,0:T(8,128)(2,1)}, f32[256,1280]{1,0:T(8,128)}, /*index=5*/f32[8,128]{1,0:T(8,128)}) custom-call(bf16[1280,256]{1,0:T(8,128)(2,1)} %get-tuple-element.31.grad_ref, bf16[1280,256]{1,0:T(8,128)(2,1)} %get-tuple-element.32.att_hbm, ...), custom_call_target="tpu_custom_call" | custom-call | flops 30000001024 | bytes 60000000 | tf_op jit(solution)/shard_map/backward/pallas_call | solution.py:1588
  253.4 0.0 copy-done
  253.4 0.0 copy-start.6
  253.4 4.6 %multiply_reduce_fusion = (f32[320]{0:T(512)S(1)}, f32[320,3840]{1,0:T(8,128)}) fusion(bf16[320,3840]{1,0:T(8,128)(2,1)S(1)} %copy-done, bf16[320,3840]{1,0:T(8,128)(2,1)} %get-tuple-element.46), kind=kLoop, calls=%fused_computation | loop fusion | flops 4914880 | bytes 9831680 | tf_op jit(solution)/shard_map/reduce_sum | solution.py:1711
  258.0 0.0 copy-start.3
  258.0 0.0 copy-start.5
  258.0 0.0 copy-done.6
  258.0 1.3 convert_element_type.32
  259.3 0.0 copy-start.4
  259.3 0.1 copy-done.3
  259.5 0.6 copy-done.5
  260.0 1.4 multiply_reduce_fusion.1
  261.4 0.0 copy-done.4
  261.4 0.0 copy-start.2
  261.4 1.3 convert_element_type.34
  262.7 0.0 copy-done.7
  262.7 0.0 copy-done.8
  262.7 0.6 convert_divide_fusion
  263.3 0.7 divide_multiply_fusion
  264.0 0.6 dynamic_slice.3
  264.6 0.0 copy-done.1
  264.6 1.1 copy.22
  265.6 0.0 copy-done.2
  265.6 1.1 copy.23
  (10 shorter events, 0.0 us)
Async XLA Ops:
  90.9 162.5 %copy-start = (bf16[320,3840]{1,0:T(8,128)(2,1)S(1)}, bf16[320,3840]{1,0:T(8,128)(2,1)}, u32[]{:S(2)}) copy-start(bf16[320,3840]{1,0:T(8,128)(2,1)} %w_ref.1) | copy-start | bytes 7372804
  253.4 4.7 %copy-start.6 = (bf16[320,1280]{1,0:T(8,128)(2,1)S(1)}, bf16[320,1280]{1,0:T(8,128)(2,1)}, u32[]{:S(2)}) copy-start(bf16[320,1280]{1,0:T(8,128)(2,1)} %get-tuple-element.47) | copy-start | bytes 2457604
  258.0 1.4 copy-start.3
  258.0 2.0 copy-start.5
  259.3 2.1 copy-start.4
  261.4 1.3 copy-start.7
  261.4 1.3 copy-start.8
  261.4 3.2 %copy-start.1 = (f32[256,1280]{1,0:T(8,128)S(1)}, f32[256,1280]{1,0:T(8,128)}, u32[]{:S(2)}) copy-start(f32[256,1280]{1,0:T(8,128)} %get-tuple-element.30) | copy-start | bytes 3932164
  261.4 4.2 %copy-start.2 = (f32[256,1280]{1,0:T(8,128)S(1)}, f32[256,1280]{1,0:T(8,128)}, u32[]{:S(2)}) copy-start(f32[256,1280]{1,0:T(8,128)} %get-tuple-element.45) | copy-start | bytes 3932164

commit v2 on v1

--- a/solution.py
+++ b/solution.py
@@ -442,6 +442,7 @@
     act_ref,
     normed_mlp_ref,
     grad_ref,
+    mult_ref,
     x_mine,
     w_mine,
     dy_mine,
@@ -646,6 +647,7 @@
     mult = jnp.where(
         real, LOG2E / math.sqrt(80) * (jnp.maximum(scale, 0.0) + jnp.log1p(jnp.exp(-jnp.abs(scale)))), 0.0
     )
+    mult_ref[...] = jnp.transpose(jnp.broadcast_to(mult, (LANES, LANES)))
     one = jnp.ones_like(mult)
     mults = jnp.concatenate([mult, mult, one, one, one, one], axis=1)
 
@@ -900,9 +902,10 @@
             shape((1280, 256), BF),
             shape((1280, 256), BF),
             shape((1280, 256), BF),
+            shape((LANES, LANES), F32),
         ),
         in_specs=[pl.BlockSpec(memory_space=pltpu.SMEM)] + [ANY_SPEC] * 2 + [VMEM_SPEC] * 2 + [ANY_SPEC] * 4,
-        out_specs=(VMEM_SPEC,) + (ANY_SPEC,) * 2 + (VMEM_SPEC,) * 4 + (ANY_SPEC,) + (VMEM_SPEC,) * 7,
+        out_specs=(VMEM_SPEC,) + (ANY_SPEC,) * 2 + (VMEM_SPEC,) * 4 + (ANY_SPEC,) + (VMEM_SPEC,) * 8,
         scratch_shapes=[
             pltpu.VMEM((256, 1280), BF),
             pltpu.VMEM((320, 3840), BF),
@@ -1404,6 +1407,10 @@
             scale_ref[...] += scale_in[stage - 1]
         if stage < 5:
             scale_copy(stage).start()
+        else:
+            given = gain_ref[2:3, :LANES]
+            soft = jnp.maximum(given, 0.0) + jnp.log1p(jnp.exp(-jnp.abs(given)))
+            scale_ref[0:1, :] = scale_ref[0:1, :] / (soft * (1.0 + jnp.exp(-given)))
 
     def norm_x(k):
         norm_copy(1, k).wait_recv()
@@ -1660,6 +1667,32 @@
     )(*args)
 
 
+def widen_kernel(*refs):
+    total = []
+    for k in range(4):
+        value = refs[k][...].astype(F32)
+        refs[6 + k][...] = value
+        if k in (0, 2):
+            total.append(jnp.sum(value * refs[4 + k // 2][...].astype(F32), axis=1, keepdims=True))
+    lane = lax.broadcasted_iota(jnp.int32, refs[10].shape, 1)
+    refs[10][...] = jnp.where(lane == 0, total[0], total[1])
+
+
+def widen(*args):
+    rows = 160
+    shape = jax.ShapeDtypeStruct
+    specs = [pl.BlockSpec((rows, a.shape[1]), lambda k: (k, 0)) for a in args]
+    return pl.pallas_call(
+        widen_kernel,
+        name="widen",
+        grid=(args[0].shape[0] // rows,),
+        out_shape=tuple(shape(a.shape, F32) for a in args[:4]) + (shape((320, LANES), F32),),
+        in_specs=specs,
+        out_specs=tuple(specs[:4]) + (pl.BlockSpec((rows, LANES), lambda k: (k, 0)),),
+        compiler_params=pltpu.CompilerParams(vmem_limit_bytes=VMEM_LIMIT),
+    )(*args)
+
+
 def fast_body(
     tokens,
     lengths,
@@ -1675,18 +1708,15 @@
 ):
     f = lax.axis_index("fsdp")
     x, dy = tokens[0], cotangent[0]
-    small = [jnp.pad(a, (0, 384 - a.shape[0])) for a in (attn_gain, mlp_gain, query_scale)]
-    small = jnp.stack(small + [jnp.zeros((384,), BF)] * 13)
+    small = jnp.zeros((16, 384), BF)
+    for k, own in enumerate((attn_gain, mlp_gain, query_scale)):
+        small = lax.dynamic_update_slice(small, own[None], (k, 0))
     (
         att_t, normed, qkv, lse, out, auxsum, place, w_heads,
-        result, resid_grad, branch_grad, up_grad, act_t, normed_mlp_t, grad_t,
+        result, resid_grad, branch_grad, up_grad, act_t, normed_mlp_t, grad_t, mult,
     ) = forward(
         lengths, x, qkv_weight, small, position, out_weight, up_weight, down_weight, dy
     )
-    scale_float = auxsum[2, :80]
-    base_scale = LOG2E / math.sqrt(80)
-    soft = jax.nn.softplus(scale_float)
-    mult = jnp.broadcast_to(jnp.pad(base_scale * soft, (0, 48))[:, None], (LANES, LANES))
     g_down, g_up, g_out, g_qkv, input_grad, scale_sum = backward(
         grad_t,
         att_t,
@@ -1706,11 +1736,9 @@
         resid_grad,
         auxsum,
     )
-    g_down, g_up, g_out = (g.astype(F32) for g in (g_down, g_up, g_out))
-    g_qkv = g_qkv.astype(F32)
-    grad_attn_gain = jnp.sum(qkv_weight.astype(F32) * g_qkv, axis=1) / attn_gain.astype(F32)
-    grad_mlp_gain = jnp.sum(up_weight.astype(F32) * g_up, axis=1) / mlp_gain.astype(F32)
-    grad_scale = scale_sum[0, :80] / soft * jax.nn.sigmoid(scale_float)
+    g_qkv, g_out, g_up, g_down, sums = widen(g_qkv, g_out, g_up, g_down, qkv_weight, up_weight)
+    grad_attn_gain = sums[:, 0] / attn_gain.astype(F32)
+    grad_mlp_gain = sums[:, 1] / mlp_gain.astype(F32)
     return (
         result[None],
         input_grad[None],
@@ -1720,7 +1748,7 @@
         g_down,
         grad_attn_gain,
         grad_mlp_gain,
-        lax.dynamic_slice_in_dim(grad_scale, f * 20, 20),
+        lax.dynamic_slice_in_dim(scale_sum[0, :80], f * 20, 20),
     )
 
 

time: 270 us -> 268 us (level)
  other arithmetic: 10.5 us -> 0.59 us
  Pallas kernels: 248 us -> 255 us
    pallas_call x0 -> x1, Pallas kernels: none -> 6.73 us  [widen(): pl.pallas_call(widen_kernel, name='widen', grid=(args[0].shape[0] // rows...]
    reduce_sum x2 -> x0, other arithmetic: 6.01 us -> none  [the longest x1 4.64 us: fast_body(): jnp.sum(qkv_weight.astype(F32) * g_qkv, axis=1) / attn_gain.astype(F32)]
where the time goes in v2:
time: 268 us; the launch traced here: 264 us
  Pallas kernels  255 us (95%)
  local copies, waits for them, and re-layouts  7.62 us (3%)
    pallas_call x1, Pallas kernels, backward(): pl.pallas_call(backward_kernel, name='backward', out_shape=(shape((320, 1...  162 us
    pallas_call x1, Pallas kernels, forward(): pl.pallas_call(attend_kernel, name='forward', out_shape=(shape((1280, 256...  85.5 us
    pallas_call x1, Pallas kernels, widen(): pl.pallas_call(widen_kernel, name='widen', grid=(args[0].shape[0] // rows...  6.73 us

profile of v2, /device:TPU:0, one launch (start us, length us, event | category | flops | bytes accessed | tf_op | source)
XLA Modules:
  0.0 264.0 jit_solution(11954917821579051159)
XLA Ops:
  0.6 0.7 broadcast_in_dim.16
  1.3 0.7 broadcast_in_dim.17
  2.0 0.1 dynamic_update_slice.10
  2.1 0.8 dynamic_update_slice.11.aux_ref
  2.9 0.0 copy-start.2
  2.9 0.6 copy-done.2
  3.5 85.5 %forward.1 = (bf16[1280,256]{1,0:T(8,128)(2,1)}, bf16[2048,1280]{1,0:T(8,128)(2,1)}, bf16[2048,768]{1,0:T(8,128)(2,1)}, f32[8,2048]{1,0:T(8,128)}, bf16[160,2048...) custom-call(s32[1,4]{1,0:T(1,128)} %ends_ref.1, ...), custom_call_target="tpu_custom_call" | custom-call | flops 20000000000 | bytes 40000000 | tf_op jit(solution)/shard_map/forward/pallas_call | solution.py:886
  89.0 162.4 %backward.1 = (bf16[320,1280]{1,0:T(8,128)(2,1)}, bf16[320,1280]{1,0:T(8,128)(2,1)}, bf16[320,1280]{1,0:T(8,128)(2,1)}, bf16[320,3840]{1,0:T(8,128)(2,1)}, f32[256,1280]{1,0:T(8,128)}, /*index=5*/f32[8,128]{1,0:T(8,128)}) custom-call(bf16[1280,256]{1,0:T(8,128)(2,1)} %get-tuple-element.37.grad_ref, bf16[1280,256]{1,0:T(8,128)(2,1)} %get-tuple-element.38.att_hbm, ...), custom_call_target="tpu_custom_call" | custom-call | flops 30000001024 | bytes 60000000 | tf_op jit(solution)/shard_map/backward/pallas_call | solution.py:1595
  251.5 0.0 copy-start.3
  251.5 0.0 copy-start.4
  251.5 0.0 copy-start
  251.5 6.7 %widen.1 = (f32[320,3840]{1,0:T(8,128)}, f32[320,1280]{1,0:T(8,128)}, f32[320,1280]{1,0:T(8,128)}, f32[320,1280]{1,0:T(8,128)}, f32[320,128]{1,0:T(8,128)}) custom-call(bf16[320,3840]{1,0:T(8,128)(2,1)} %get-tuple-element.53.refs_0_, bf16[320,1280]{1,0:T(8,128)(2,1)} %get-tuple-element.54.refs_1_, bf16[320,1280]{1,0:T(8,128)(2,1)} %get-tuple-element.55.refs_2_, ...), custom_call_target="tpu_custom_call" | custom-call | tf_op jit(solution)/shard_map/widen/pallas_call | solution.py:1685
  258.2 0.0 copy-start.1
  258.2 1.4 slice_reduce_fusion
  259.6 0.0 copy-done.3
  259.6 0.0 copy-done.4
  259.6 0.6 convert_divide_fusion
  260.2 0.7 slice.11
  260.9 0.6 dynamic-slice_bitcast_fusion
  261.5 0.0 copy-done
  261.5 1.1 copy.24
  262.5 0.0 copy-done.1
  262.5 1.1 copy.25
  (1 shorter events, 0.0 us)
Async XLA Ops:
  2.9 0.6 copy-start.2
  251.5 8.1 %copy-start.3 = (bf16[320]{0:T(512)(128)(2,1)S(1)}, bf16[320]{0:T(512)(128)(2,1)}, u32[]{:S(2)}) copy-start(bf16[320]{0:T(512)(128)(2,1)} %param.18) | copy-start | bytes 1924
  251.5 8.1 %copy-start.4 = (bf16[320]{0:T(512)(128)(2,1)S(1)}, bf16[320]{0:T(512)(128)(2,1)}, u32[]{:S(2)}) copy-start(bf16[320]{0:T(512)(128)(2,1)} %param.19) | copy-start | bytes 1924
  251.5 10.0 %copy-start = (f32[256,1280]{1,0:T(8,128)S(1)}, f32[256,1280]{1,0:T(8,128)}, u32[]{:S(2)}) copy-start(f32[256,1280]{1,0:T(8,128)} %get-tuple-element.36) | copy-start | bytes 3932164
  258.2 4.3 %copy-start.1 = (f32[256,1280]{1,0:T(8,128)S(1)}, f32[256,1280]{1,0:T(8,128)}, u32[]{:S(2)}) copy-start(f32[256,1280]{1,0:T(8,128)} %get-tuple-element.52) | copy-start | bytes 3932164

commit v3 on v2

--- a/solution.py
+++ b/solution.py
@@ -427,20 +427,20 @@
     up_w_ref,
     down_w_ref,
     dy_ref,
-    att_ref,
+    att_save,
     normed_out,
     qkv_out,
     lse_ref,
-    out_ref,
+    out_save,
     auxsum_ref,
     place_ref,
     w_out,
     result_ref,
-    resid_grad_ref,
-    branch_ref,
-    up_grad_ref,
-    act_ref,
-    normed_mlp_ref,
+    resid_grad_save,
+    branch_save,
+    up_grad_save,
+    act_save,
+    normed_mlp_save,
     grad_ref,
     mult_ref,
     x_mine,
@@ -472,7 +472,29 @@
     local_sem,
     save_sem,
     shard_sem,
+    att_ref,
+    out_ref,
+    resid_grad_ref,
+    branch_ref,
+    up_grad_ref,
+    act_ref,
+    normed_mlp_ref,
+    early_sem,
 ):
+    early = {
+        name: pltpu.make_async_copy(src, dst, early_sem.at[k])
+        for k, (name, src, dst) in enumerate(
+            (
+                ("att", att_ref, att_save),
+                ("out", out_ref, out_save),
+                ("resid_grad", resid_grad_ref, resid_grad_save),
+                ("branch", branch_ref, branch_save),
+                ("up_grad", up_grad_ref, up_grad_save),
+                ("act", act_ref, act_save),
+                ("normed_mlp", normed_mlp_ref, normed_mlp_save),
+            )
+        )
+    }
     w_load = pltpu.make_async_copy(w_ref, w_mine, local_sem.at[0])
     w_load.start()
     x_load = pltpu.make_async_copy(x_ref, x_mine, local_sem.at[2])
@@ -689,11 +711,11 @@
                 def _(way=way, where=where, onward=onward):
                     onward(way, where)
 
-        @pl.when(step == 3)
+        @pl.when(step == 2)
         def _():
             weight_first(0)
 
-        @pl.when(step == 5)
+        @pl.when(step == 4)
         def _():
             weight_first(1)
 
@@ -799,6 +821,7 @@
 
     lax.fori_loop(0, 8, attend, 0)
     weight_second(2)
+    early["out"].start()
     lse_ref[2:8, :] = jnp.zeros((6, 2048), F32)
 
     def land(block, carry):
@@ -814,6 +837,7 @@
 
     weight_last(0)
     lax.fori_loop(0, 8, land, 0)
+    early["att"].start()
 
     def across(left, right):
         return lax.dot_general(
@@ -827,27 +851,34 @@
     inv = lax.rsqrt(jnp.mean(resid * resid, axis=1, keepdims=True) + EPS)
     normed_mlp = (resid * inv * mlp_gain).astype(BF)
     normed_mlp_ref[...] = jnp.transpose(normed_mlp)
+    early["normed_mlp"].start()
     weight_last(1)
     up = jnp.dot(normed_mlp, weights[1], preferred_element_type=F32)
     sigma = 1.0 / (1.0 + jnp.exp(-up))
     act = (up * sigma).astype(BF)
     act_ref[...] = jnp.transpose(act)
+    early["act"].start()
     slope = sigma * (1.0 + up * (1.0 - sigma))
     weight_last(2)
     dy = dy_mine[...]
     up_grad = (across(dy, weights[2]) * slope).astype(BF)
     up_grad_ref[...] = up_grad
+    early["up_grad"].start()
     scaled = across(up_grad, weights[1]) * mlp_gain
     resid_grad = dy.astype(F32) + inv * (
         scaled - resid * inv * inv * jnp.mean(scaled * resid, axis=1, keepdims=True)
     )
     resid_grad_ref[...] = resid_grad
+    early["resid_grad"].start()
     branch = resid_grad.astype(BF)
     branch_ref[...] = branch
+    early["branch"].start()
     grad_ref[...] = across(weights[0], branch).astype(BF)
     result_ref[...] = resid + jnp.dot(act, weights[2], preferred_element_type=F32)
 
     w_save.wait()
+    for copy in early.values():
+        copy.wait()
     for k in range(8):
         rows = pl.ds(k * 256, 256)
         pltpu.make_async_copy(normed_ref.at[rows], normed_out.at[rows], save_sem.at[k, 0]).wait()
@@ -905,7 +936,10 @@
             shape((LANES, LANES), F32),
         ),
         in_specs=[pl.BlockSpec(memory_space=pltpu.SMEM)] + [ANY_SPEC] * 2 + [VMEM_SPEC] * 2 + [ANY_SPEC] * 4,
-        out_specs=(VMEM_SPEC,) + (ANY_SPEC,) * 2 + (VMEM_SPEC,) * 4 + (ANY_SPEC,) + (VMEM_SPEC,) * 8,
+        out_specs=(ANY_SPEC,) * 3
+        + (VMEM_SPEC, ANY_SPEC, VMEM_SPEC, VMEM_SPEC, ANY_SPEC, VMEM_SPEC)
+        + (ANY_SPEC,) * 5
+        + (VMEM_SPEC,) * 2,
         scratch_shapes=[
             pltpu.VMEM((256, 1280), BF),
             pltpu.VMEM((320, 3840), BF),
@@ -936,6 +970,14 @@
             dma((6,)),
             dma((8, 2)),
             dma((3,)),
+            pltpu.VMEM((1280, 256), BF),
+            pltpu.VMEM((160, 2048), BF),
+            pltpu.VMEM((256, 1280), F32),
+            pltpu.VMEM((256, 1280), BF),
+            pltpu.VMEM((256, 1280), BF),
+            pltpu.VMEM((1280, 256), BF),
+            pltpu.VMEM((1280, 256), BF),
+            dma((7,)),
         ],
         compiler_params=pltpu.CompilerParams(
             collective_id=0, has_side_effects=True, vmem_limit_bytes=VMEM_LIMIT
@@ -1250,18 +1292,20 @@
 
     def head_copy(stage, h):
         if stage == 0:
-            src, dst, to = slices.at[h, :, span((1 - row) * 640, 640, 640)], s1.at[h], across
+            rows = pl.ds(0, 240)
+            src, to = slices.at[h, rows, span((1 - row) * 640, 640, 640)], across
+            dst = s1.at[h, rows]
         elif stage == 1:
             src, dst, to = s1.at[h, span(128 - half * 128, 128, 128)], s2.at[h], hpeer
         elif stage < 5:
             way = HEAD_WAYS[stage - 2]
             known = HEAD_WAYS[: stage - 2]
             where = (core,) + tuple(slice(None) if d in known else bits[d] for d in "xz") + (h,)
-            rows = slice(None) if "h" in known else span(half * 128, 128, 128)
+            rows = pl.ds(0, 240) if "h" in known else span(half * 128, 128, 128)
             src = dst = gathered.at[where + (rows,)]
             to = peers[way]
         else:
-            src = dst = gathered.at[core, :, :, h]
+            src = dst = gathered.at[core, :, :, h, pl.ds(0, 240)]
             to = twin
         return remote(src, dst, q_send.at[stage, h], q_recv.at[stage, h], to)
 
@@ -1336,6 +1380,7 @@
 
     def head_first(h):
         slices[h, 240:, :] = jnp.zeros((16, 1280), BF)
+        s1[h, 240:, :] = jnp.zeros((16, 640), BF)
         for part in range(5):
             normed_load(part).wait()
             if part + 1 < 5:

time: 268 us -> 265 us (0.989)
  Pallas kernels: 255 us -> 252 us
where the time goes in v3:
time: 265 us; the launch traced here: 262 us
  Pallas kernels  252 us (95%)
  local copies, waits for them, and re-layouts  7.62 us (3%)
    pallas_call x1, Pallas kernels, backward(): pl.pallas_call(backward_kernel, name='backward', out_shape=(shape((320, 1...  161 us
    pallas_call x1, Pallas kernels, forward(): pl.pallas_call(attend_kernel, name='forward', out_shape=(shape((1280, 256...  84 us
    pallas_call x1, Pallas kernels, widen(): pl.pallas_call(widen_kernel, name='widen', grid=(args[0].shape[0] // rows...  6.73 us

profile of v3, /device:TPU:0, one launch (start us, length us, event | category | flops | bytes accessed | tf_op | source)
XLA Modules:
  0.0 261.6 jit_solution(7107641535114045564)
XLA Ops:
  0.6 0.7 broadcast_in_dim.16
  1.3 0.7 broadcast_in_dim.17
  2.0 0.1 dynamic_update_slice.10
  2.1 0.8 dynamic_update_slice.11.aux_ref
  2.9 0.0 copy-start.2
  2.9 0.6 copy-done.2
  3.5 84.0 %forward.1 = (bf16[1280,256]{1,0:T(8,128)(2,1)}, bf16[2048,1280]{1,0:T(8,128)(2,1)}, bf16[2048,768]{1,0:T(8,128)(2,1)}, f32[8,2048]{1,0:T(8,128)}, bf16[160,2048...) custom-call(s32[1,4]{1,0:T(1,128)} %ends_ref.1, ...), custom_call_target="tpu_custom_call" | custom-call | flops 20000000000 | bytes 40000000 | tf_op jit(solution)/shard_map/forward/pallas_call | solution.py:917
  87.6 161.5 %backward.1 = (bf16[320,1280]{1,0:T(8,128)(2,1)}, bf16[320,1280]{1,0:T(8,128)(2,1)}, bf16[320,1280]{1,0:T(8,128)(2,1)}, bf16[320,3840]{1,0:T(8,128)(2,1)}, f32[256,1280]{1,0:T(8,128)}, /*index=5*/f32[8,128]{1,0:T(8,128)}) custom-call(bf16[1280,256]{1,0:T(8,128)(2,1)} %get-tuple-element.37.grad_ref, bf16[1280,256]{1,0:T(8,128)(2,1)} %get-tuple-element.38.att_hbm, ...), custom_call_target="tpu_custom_call" | custom-call | flops 30000001024 | bytes 60000000 | tf_op jit(solution)/shard_map/backward/pallas_call | solution.py:1640
  249.1 0.0 copy-start.3
  249.1 0.0 copy-start.4
  249.1 0.0 copy-start
  249.1 6.7 %widen.1 = (f32[320,3840]{1,0:T(8,128)}, f32[320,1280]{1,0:T(8,128)}, f32[320,1280]{1,0:T(8,128)}, f32[320,1280]{1,0:T(8,128)}, f32[320,128]{1,0:T(8,128)}) custom-call(bf16[320,3840]{1,0:T(8,128)(2,1)} %get-tuple-element.53.refs_0_, bf16[320,1280]{1,0:T(8,128)(2,1)} %get-tuple-element.54.refs_1_, bf16[320,1280]{1,0:T(8,128)(2,1)} %get-tuple-element.55.refs_2_, ...), custom_call_target="tpu_custom_call" | custom-call | tf_op jit(solution)/shard_map/widen/pallas_call | solution.py:1730
  255.8 0.0 copy-start.1
  255.8 1.4 slice_reduce_fusion
  257.2 0.0 copy-done.3
  257.2 0.0 copy-done.4
  257.2 0.6 convert_divide_fusion
  257.8 0.7 slice.11
  258.5 0.6 dynamic-slice_bitcast_fusion
  259.1 0.0 copy-done
  259.1 1.1 copy.24
  260.1 0.0 copy-done.1
  260.1 1.1 copy.25
  (1 shorter events, 0.0 us)
Async XLA Ops:
  2.9 0.6 copy-start.2
  249.1 8.1 %copy-start.3 = (bf16[320]{0:T(512)(128)(2,1)S(1)}, bf16[320]{0:T(512)(128)(2,1)}, u32[]{:S(2)}) copy-start(bf16[320]{0:T(512)(128)(2,1)} %param.18) | copy-start | bytes 1924
  249.1 8.1 %copy-start.4 = (bf16[320]{0:T(512)(128)(2,1)S(1)}, bf16[320]{0:T(512)(128)(2,1)}, u32[]{:S(2)}) copy-start(bf16[320]{0:T(512)(128)(2,1)} %param.19) | copy-start | bytes 1924
  249.1 10.0 %copy-start = (f32[256,1280]{1,0:T(8,128)S(1)}, f32[256,1280]{1,0:T(8,128)}, u32[]{:S(2)}) copy-start(f32[256,1280]{1,0:T(8,128)} %get-tuple-element.36) | copy-start | bytes 3932164
  255.8 4.3 %copy-start.1 = (f32[256,1280]{1,0:T(8,128)S(1)}, f32[256,1280]{1,0:T(8,128)}, u32[]{:S(2)}) copy-start(f32[256,1280]{1,0:T(8,128)} %get-tuple-element.52) | copy-start | bytes 3932164

commit v4 on v3

--- a/solution.py
+++ b/solution.py
@@ -998,7 +998,7 @@
 
 
 SUM_WAYS = ("yxzh", "zyxh", "zxyh")
-SPREAD_WAYS = ("zhx", "hxz", "hxz")
+SPREAD_WAYS = ("hzx", "hxz", "hxz")
 HEAD_WAYS = "hzx"
 
 PLAN = (

time: 265 us -> 265 us (level)
  no operation moved by 1% of the time
where the time goes in v4:
time: 265 us; the launch traced here: 262 us
  Pallas kernels  252 us (95%)
  local copies, waits for them, and re-layouts  7.62 us (3%)
    pallas_call x1, Pallas kernels, backward(): pl.pallas_call(backward_kernel, name='backward', out_shape=(shape((320, 1...  161 us
    pallas_call x1, Pallas kernels, forward(): pl.pallas_call(attend_kernel, name='forward', out_shape=(shape((1280, 256...  84 us
    pallas_call x1, Pallas kernels, widen(): pl.pallas_call(widen_kernel, name='widen', grid=(args[0].shape[0] // rows...  6.73 us

profile of v4, /device:TPU:0, one launch (start us, length us, event | category | flops | bytes accessed | tf_op | source)
XLA Modules:
  0.0 261.6 jit_solution(7838379477274323384)
XLA Ops:
  0.6 0.7 broadcast_in_dim.16
  1.3 0.7 broadcast_in_dim.17
  2.0 0.1 dynamic_update_slice.10
  2.1 0.8 dynamic_update_slice.11.aux_ref
  2.9 0.0 copy-start.2
  2.9 0.6 copy-done.2
  3.5 84.0 %forward.1 = (bf16[1280,256]{1,0:T(8,128)(2,1)}, bf16[2048,1280]{1,0:T(8,128)(2,1)}, bf16[2048,768]{1,0:T(8,128)(2,1)}, f32[8,2048]{1,0:T(8,128)}, bf16[160,2048...) custom-call(s32[1,4]{1,0:T(1,128)} %ends_ref.1, ...), custom_call_target="tpu_custom_call" | custom-call | flops 20000000000 | bytes 40000000 | tf_op jit(solution)/shard_map/forward/pallas_call | solution.py:917
  87.6 161.5 %backward.1 = (bf16[320,1280]{1,0:T(8,128)(2,1)}, bf16[320,1280]{1,0:T(8,128)(2,1)}, bf16[320,1280]{1,0:T(8,128)(2,1)}, bf16[320,3840]{1,0:T(8,128)(2,1)}, f32[256,1280]{1,0:T(8,128)}, /*index=5*/f32[8,128]{1,0:T(8,128)}) custom-call(bf16[1280,256]{1,0:T(8,128)(2,1)} %get-tuple-element.37.grad_ref, bf16[1280,256]{1,0:T(8,128)(2,1)} %get-tuple-element.38.att_hbm, ...), custom_call_target="tpu_custom_call" | custom-call | flops 30000001024 | bytes 60000000 | tf_op jit(solution)/shard_map/backward/pallas_call | solution.py:1640
  249.1 0.0 copy-start.3
  249.1 0.0 copy-start.4
  249.1 0.0 copy-start
  249.1 6.7 %widen.1 = (f32[320,3840]{1,0:T(8,128)}, f32[320,1280]{1,0:T(8,128)}, f32[320,1280]{1,0:T(8,128)}, f32[320,1280]{1,0:T(8,128)}, f32[320,128]{1,0:T(8,128)}) custom-call(bf16[320,3840]{1,0:T(8,128)(2,1)} %get-tuple-element.53.refs_0_, bf16[320,1280]{1,0:T(8,128)(2,1)} %get-tuple-element.54.refs_1_, bf16[320,1280]{1,0:T(8,128)(2,1)} %get-tuple-element.55.refs_2_, ...), custom_call_target="tpu_custom_call" | custom-call | tf_op jit(solution)/shard_map/widen/pallas_call | solution.py:1730
  255.8 0.0 copy-start.1
  255.8 1.4 slice_reduce_fusion
  257.2 0.0 copy-done.3
  257.2 0.0 copy-done.4
  257.2 0.6 convert_divide_fusion
  257.8 0.7 slice.11
  258.5 0.6 dynamic-slice_bitcast_fusion
  259.1 0.0 copy-done
  259.1 1.1 copy.24
  260.1 0.0 copy-done.1
  260.1 1.1 copy.25
  (1 shorter events, 0.0 us)
Async XLA Ops:
  2.9 0.6 copy-start.2
  249.1 8.1 %copy-start.3 = (bf16[320]{0:T(512)(128)(2,1)S(1)}, bf16[320]{0:T(512)(128)(2,1)}, u32[]{:S(2)}) copy-start(bf16[320]{0:T(512)(128)(2,1)} %param.18) | copy-start | bytes 1924
  249.1 8.1 %copy-start.4 = (bf16[320]{0:T(512)(128)(2,1)S(1)}, bf16[320]{0:T(512)(128)(2,1)}, u32[]{:S(2)}) copy-start(bf16[320]{0:T(512)(128)(2,1)} %param.19) | copy-start | bytes 1924
  249.1 10.0 %copy-start = (f32[256,1280]{1,0:T(8,128)S(1)}, f32[256,1280]{1,0:T(8,128)}, u32[]{:S(2)}) copy-start(f32[256,1280]{1,0:T(8,128)} %get-tuple-element.36) | copy-start | bytes 3932164
  255.8 4.3 %copy-start.1 = (f32[256,1280]{1,0:T(8,128)S(1)}, f32[256,1280]{1,0:T(8,128)}, u32[]{:S(2)}) copy-start(f32[256,1280]{1,0:T(8,128)} %get-tuple-element.52) | copy-start | bytes 3932164
